TPU v7x, 512 devices: a whole 4x4x16 slice. The times are simulated.
512 devices in a mesh: wide: 64 (over z, x), col: 8 (over y, core).
Axes of the slice: x: 4, y: 4, z: 16, core: 2. Of those that a mesh axis runs over, the one named last changes fastest.
Arguments:
- phi_values: bfloat16 [64, 8, 8, 384, 512], P('wide', 'col'), may hold values from -1.5 to 1.5
- density: bfloat16 [128, 16, 128, 128], P('wide', 'col'), may hold values from -3.5 to 3.5
- lnv_matrix: bfloat16 [128, 16, 128, 128], P('wide', 'col'), may hold values from -0.1875 to 0.1875
- core_density: float32 [128, 128, 128], P('wide', 'col'), may hold values from 0.5 to 2
- pair_owner: int32 [64, 8, 72, 1], P('wide', 'col'), may hold values from 0 to 63; in each aligned block of 72 rows (0 to 71, 72 to 143, ..., all dimensions but the last counted through in order) at most 2 rows name the same one
- pair_source: int32 [64, 8, 72], P('wide', 'col'), may hold values from 0 to 3
- term_left: int32 [128, 16, 8], P('wide', 'col'), may hold values from 0 to 15
- term_right: int32 [128, 16, 8], P('wide', 'col'), may hold values from 0 to 11
Outputs:
- potential: float32 [128, 128, 128], P('wide', 'col')
- hamiltonian: float32 [128, 16, 128, 128], P('wide', 'col')
- gradient: float32 [128, 16, 128, 128], P('wide', 'col')
Inputs may be any that keep to these rules, and one draw needn't show every extreme that they name: `pair_owner`: within the 72 pairs of one device no owner is named more than 2 times, and some device names some owner exactly 2 times.
All inputs are finite; a program needn't handle non-finite values.
Results may differ from a plain program's by a relative error of at most 0.0051.
Values may be sent and summed in bfloat16 or wider, within the bound.
A program may use at most 64 MiB of HBM per device.

v0:
```python
import jax
import jax.numpy as jnp
from jax import lax
from jax.sharding import Mesh
from jax.sharding import PartitionSpec as P

WIDE = ("wide_0", "wide_1")


SPACING = 0.1
ENHANCE_LIMIT = 0.804
GRADIENT_COEFF = 0.2195


def in_blocks(array, dim, size):
    dims = array.shape
    blocks = array.reshape(*dims[:dim], size, dims[dim] // size, *dims[dim + 1 :])
    return jnp.moveaxis(blocks, dim, 0)


def joined_along(blocks, dim):
    dims = list(blocks.shape[1:])
    dims[dim] *= blocks.shape[0]
    return jnp.moveaxis(blocks, 0, dim).reshape(dims)


def turned_blocks(blocks, axes, order):
    dims = [lax.axis_size(a) for a in axes]
    blocks = blocks.reshape(*dims, *blocks.shape[1:])
    for k in order:
        blocks = lax.all_to_all(blocks, axes[k], split_axis=k, concat_axis=k, tiled=True)
    return blocks.reshape(-1, *blocks.shape[len(axes) :])


def one_axis_at_a_time(array, axes, order, split_dim, concat_dim):
    blocks = in_blocks(array, split_dim, lax.axis_size(axes))
    return joined_along(turned_blocks(blocks, axes, order), concat_dim)


def gathered_by_axis(array, axes, dim):
    result = array
    for number in range(len(axes) - 1, -1, -1):
        result = lax.all_gather(result, axes[number], axis=dim, tiled=True)
    return result


def padded_2(cells, sides, width):
    for axis, dim in sides:
        count = lax.axis_size(axis)
        head = lax.slice_in_dim(cells, 0, width, axis=dim)
        tail = lax.slice_in_dim(cells, cells.shape[dim] - width, cells.shape[dim], axis=dim)
        cells = jnp.concatenate(
            [
                lax.ppermute(tail, axis, [(i, (i + 1) % count) for i in range(count)]),
                cells,
                lax.ppermute(head, axis, [((i + 1) % count, i) for i in range(count)]),
            ],
            axis=dim,
        )
    return cells


def with_halo(array, sides, width):
    edges = {}
    for axis, dim in sides:
        size, length = (lax.axis_size(axis), array.shape[dim])
        up = [(i, (i + 1) % size) for i in range(size)]
        last = lax.slice_in_dim(array, length - width, length, axis=dim)
        first = lax.slice_in_dim(array, 0, width, axis=dim)
        edges[dim] = (
            lax.ppermute(last, axis, up),
            lax.ppermute(first, axis, [(b, a) for a, b in up]),
        )
    done = []
    for _, dim in sides:
        low, high = edges[dim]
        around = [(width, width) if d in done else (0, 0) for d in range(array.ndim)]
        array = jnp.concatenate([jnp.pad(low, around), array, jnp.pad(high, around)], axis=dim)
        done.append(dim)
    return array


def sent_to_all(array, axis):
    size = lax.axis_size(axis)
    return lax.all_to_all(
        jnp.broadcast_to(array[None], (size, *array.shape)), axis, 0, 0, tiled=True
    )


def gather_directly(array, axis, dim):
    blocks = sent_to_all(array, axis)
    return joined_along(blocks, dim)


def exchange_energy(smooth, grad_sq):
    fermi_sq = (3.0 * jnp.pi**2) ** (2.0 / 3.0)
    reduced = grad_sq / (4.0 * fermi_sq * smooth ** (8.0 / 3.0))
    enhance = 1.0 + ENHANCE_LIMIT - ENHANCE_LIMIT / (1.0 + GRADIENT_COEFF * reduced / ENHANCE_LIMIT)
    return -0.75 * (3.0 / jnp.pi) ** (1.0 / 3.0) * smooth ** (4.0 / 3.0) * enhance


def cell_terms(charge, core_values, grad_first, grad_second):
    grad_third = (jnp.roll(charge, -1, 2) - jnp.roll(charge, 1, 2)) / (2.0 * SPACING)
    smooth = jnp.sqrt(charge * charge + core_values * core_values)
    grad_sq = grad_first * grad_first + grad_second * grad_second + grad_third * grad_third
    energy, pullback = jax.vjp(exchange_energy, smooth, grad_sq)
    slope_smooth, slope_grad = pullback(jnp.ones_like(energy))
    local_part = slope_smooth * charge / smooth
    return (
        local_part,
        2.0 * slope_grad * grad_first,
        2.0 * slope_grad * grad_second,
        2.0 * slope_grad * grad_third,
    )


def body(
    phi_values, density, lnv_matrix, core_density, pair_owner, pair_source, term_left, term_right
):
    orbital_values = phi_values[0, 0]
    tile_count = orbital_values.shape[0]
    block_width = orbital_values.shape[1] // 3
    block_rows, slot_count = (density.shape[0], density.shape[1])
    local_count = block_rows * slot_count
    slab_cells, strip_cells, depth_cells = core_density.shape
    depth_tile = depth_cells // tile_count
    owners = pair_owner[0, 0, :, 0]
    sources = pair_source[0, 0]
    pair_count = owners.shape[0]
    slab_count = lax.axis_size(WIDE)
    capacity = max(2, 3 * pair_count // (2 * slab_count))
    owner_hits = (owners[:, None] == jnp.arange(slab_count, dtype=jnp.int32)[None, :]).astype(
        jnp.int32
    )
    before = jnp.cumsum(owner_hits, axis=0) - owner_hits
    seat_index = owners * capacity + jnp.sum(before * owner_hits, axis=1)
    placing = seat_index[:, None] == jnp.arange(slab_count * capacity, dtype=jnp.int32)[None, :]
    asked = jnp.sum(jnp.where(placing, sources[:, None] + 1, 0), axis=0) - 1
    wanted = one_axis_at_a_time(asked.reshape(slab_count, capacity), WIDE, (0, 1), 0, 0).reshape(
        slab_count * capacity
    )
    local_blocks = density.reshape(local_count, block_width, block_width)
    gathered = gathered_by_axis(local_blocks, WIDE, 0)
    blocks = gathered[owners * local_count + sources]
    tile_matrix = (
        blocks.reshape(tile_count, 3, 3, block_width, block_width)
        .transpose(0, 1, 3, 2, 4)
        .reshape(tile_count, 3 * block_width, 3 * block_width)
    )
    applied = jnp.einsum(
        "tij,tjp->tip", tile_matrix, orbital_values, preferred_element_type=jnp.float32
    )
    tile_charge = jnp.sum(orbital_values * applied, axis=1)
    charge = (
        tile_charge.reshape(tile_count, slab_cells, strip_cells, depth_tile)
        .transpose(1, 2, 0, 3)
        .reshape(slab_cells, strip_cells, depth_cells)
    )
    padded = padded_2(charge, ((WIDE, 0), ("col", 1)), 1)
    grad_first = (padded[2:, 1:-1] - padded[:-2, 1:-1]) / (2.0 * SPACING)
    grad_second = (padded[1:-1, 2:] - padded[1:-1, :-2]) / (2.0 * SPACING)
    local_part, flux_first, flux_second, flux_third = cell_terms(
        charge, core_density, grad_first, grad_second
    )
    fluxes = with_halo(jnp.stack([flux_first, flux_second]), ((WIDE, 1), ("col", 2)), 1)
    rim_first = fluxes[0]
    rim_second = fluxes[1]
    divergence = (
        rim_first[:-2, 1:-1] - rim_first[2:, 1:-1] + rim_second[1:-1, :-2] - rim_second[1:-1, 2:]
    )
    divergence = divergence + jnp.roll(flux_third, 1, 2) - jnp.roll(flux_third, -1, 2)
    potential = local_part + divergence / (2.0 * SPACING)
    voltage = (
        potential.reshape(slab_cells, strip_cells, tile_count, depth_tile)
        .transpose(2, 0, 1, 3)
        .reshape(tile_count, -1)
    )
    weighted = (orbital_values * voltage[:, None, :]).astype(jnp.bfloat16)
    tile_ham = jnp.einsum(
        "tip,tjp->tij", weighted, orbital_values, preferred_element_type=jnp.float32
    )
    pieces = tile_ham.reshape(tile_count, 3, block_width, 3, block_width).transpose(0, 1, 3, 2, 4)
    pieces = pieces.reshape(pair_count, block_width * block_width).astype(jnp.bfloat16)
    outgoing_parts = jnp.einsum(
        "qk,qm->km", placing.astype(jnp.bfloat16), pieces, preferred_element_type=jnp.float32
    ).astype(jnp.bfloat16)
    returned = lax.all_to_all(
        outgoing_parts.reshape(slab_count, capacity, block_width * block_width),
        WIDE,
        split_axis=0,
        concat_axis=0,
        tiled=True,
    )
    picking = (wanted[None, :] == jnp.arange(local_count, dtype=jnp.int32)[:, None]).astype(
        jnp.bfloat16
    )
    ham_flat = jnp.dot(
        picking,
        returned.reshape(slab_count * capacity, block_width * block_width),
        preferred_element_type=jnp.float32,
    )
    hamiltonian = ham_flat.reshape(block_rows, slot_count, block_width, block_width)
    full_rows = gather_directly(lnv_matrix, "col", 1)
    total_slots = full_rows.shape[1]
    term_count = term_left.shape[2]
    left_index = (
        jnp.arange(block_rows, dtype=jnp.int32)[:, None, None] * total_slots + term_left
    ).reshape(-1)
    chosen_left = full_rows.reshape(block_rows * total_slots, block_width, block_width)[left_index]
    chosen_left = chosen_left.reshape(local_count, term_count, block_width, block_width)

    def product(right_blocks):
        window = padded_2(right_blocks, ((WIDE, 0),), block_rows)
        chosen_right = window.reshape(3 * local_count, block_width, block_width)[
            term_right.reshape(-1)
        ]
        chosen_right = chosen_right.reshape(local_count, term_count, block_width, block_width)
        summed = jnp.einsum(
            "jtab,jtbc->jac", chosen_left, chosen_right, preferred_element_type=jnp.float32
        )
        return summed.reshape(block_rows, slot_count, block_width, block_width)

    first_term = product(hamiltonian.astype(jnp.bfloat16))
    second = product(first_term.astype(jnp.bfloat16))
    gradient = 3.0 * first_term - 2.0 * second
    return (potential, hamiltonian, gradient)


def solution(mesh):
    split = Mesh(mesh.devices.reshape(16, 4, mesh.shape["col"]), ("wide_0", "wide_1", "col"))
    in_specs = (
        P(WIDE, "col", None, None, None),
        P(WIDE, "col", None, None),
        P(WIDE, "col", None, None),
        P(WIDE, "col", None),
        P(WIDE, "col", None, None),
        P(WIDE, "col", None),
        P(WIDE, "col", None),
        P(WIDE, "col", None),
    )
    out_specs = (P(WIDE, "col", None), P(WIDE, "col", None, None), P(WIDE, "col", None, None))
    return jax.shard_map(body, mesh=split, in_specs=in_specs, out_specs=out_specs, check_vma=False)
```

profile of v0, /device:TPU:24, one launch (start us, length us, event | category | flops | bytes accessed | tf_op | source)
XLA Modules:
  0.0 462.3 jit_solution(17212314033065257470)
XLA Ops:
  7.2 14.8 %all_gather.6 = bf16[16,128,128]{2,1,0:T(8,128)(2,1)} all-gather(bf16[4,128,128]{2,1,0:T(8,128)(2,1)} %bitcast.116), channel_id=1, replica_groups=mesh['wide_0'=16,'wide_1'=4,'col'=8] {'wide_1'}, dimensions={0}, use_global_device_ids=true | all-gather | bytes 655360 | tf_op jit(solution)/shard_map/all_gather | solution.py:43
  22.0 0.7 fusion.19
  22.7 0.1 reduce_window_sum.11
  22.8 0.8 select_reduce_fusion.1
  23.7 0.7 add_bitcast_fusion
  24.3 0.7 multiply_add_fusion.3
  25.0 0.1 select_reduce_fusion
  25.1 0.2 sub.49
  25.3 0.8 copy.46
  26.1 15.2 %all-to-all-start = ((s32[16,4,1,2]{1,3,2,0:T(2,128)}), s32[16,4,1,2]{1,3,2,0:T(2,128)S(1)}, u32[]{:S(2)}, u32[]{:S(2)}) async-start(s32[16,4,1,2]{1,3,2,0:T(2,128)} %copy.46), calls=%async_computation | async-start | bytes 32768 | tf_op jit(solution)/shard_map/all_to_all | solution.py:31
  41.3 0.7 fusion.37
  42.0 11.9 %all-to-all-done = s32[16,4,1,2]{1,3,2,0:T(2,128)S(1)} async-done(((s32[16,4,1,2]{1,3,2,0:T(2,128)}), s32[16,4,1,2]{1,3,2,0:T(2,128)S(1)}, u32[]{:S(2)}, u32[]{:S(2)}) %all-to-all-start) | async-done | bytes 544 | tf_op jit(solution)/shard_map/all_to_all | solution.py:31
  53.9 0.7 copy.47
  54.6 3.2 all-to-all-start.1
  57.9 73.6 %all-gather.2.cloned.1.call-done = bf16[256,128,128]{2,1,0:T(8,128)(2,1)} async-done(((bf16[16,128,128]{2,1,0:T(8,128)(2,1)}), bf16[256,128,128]{2,1,0:T(8,128)(2,1)}) %all-gather.2.cloned.1.call-update) | async-done | bytes 8388624 | tf_op jit(solution)/shard_map/all_gather | solution.py:43
  131.4 5.9 %gather_fusion = bf16[72,128,128]{2,1,0:T(8,128)(2,1)} fusion(bf16[256,128,128]{2,1,0:T(8,128)(2,1)} %all-gather.2.cloned.1.call-done, s32[1024]{0:T(1024)S(1)} %pad_clamp_fusion.2), kind=kCustom, calls=%fused_computation | custom fusion | bytes 4718880 | tf_op jit(solution)/shard_map/gather | solution.py:144
  137.3 3.8 copy.42
  141.1 4.1 reshape.213
  145.3 5.3 %fusion = f32[8,512]{1,0:T(8,128)S(1)} fusion(bf16[1,1,8,384,512]{4,3,2,1,0:T(8,128)(2,1)} %param.8, bf16[8,384,384]{2,1,0:T(8,128)(2,1)} %reshape.213), kind=kOutput, calls=%fused_computation.7 | convolution fusion | flops 1212674048 | bytes 5521408 | tf_op jit(solution)/shard_map/tij,tjp->tip/dot_general | solution.py:150
  150.6 0.1 reshape.214
  150.8 0.1 reshape.215
  151.1 3.3 collective-permute-start.1
  154.5 5.9 %collective-permute-start = (f32[1,16,128]{2,1,0:T(8,128)S(1)}, f32[1,16,128]{2,1,0:T(8,128)S(1)}, u32[]{:S(2)}, u32[]{:S(2)}) collective-permute-start(f32[1,16,128]{2,1,0:T(8,128)S(1)} %slice.93), channel_id=1, source_target_pairs={{8,0},{16,8},{24,16},{32,24},{40,32},{48,40},{56,48},{64,56},{72,6... | collective-permute-start | bytes 24584 | tf_op jit(solution)/shard_map/ppermute | solution.py:56
  160.4 1.3 collective-permute-done
  161.7 0.5 collective-permute-start.3
  162.3 0.7 collective-permute-done.2
  163.0 1.7 collective-permute-done.3
  164.7 0.1 fusion.40
  164.9 1.9 collective-permute-start.5
  166.8 7.5 %collective-permute-start.6 = (f32[2,1,16,128]{3,2,1,0:T(8,128)S(1)}, f32[2,1,16,128]{3,2,1,0:T(8,128)S(1)}, u32[]{:S(2)}, u32[]{:S(2)}) collective-permute-start(f32[2,1,16,128]{3,2,1,0:T(8,128)S(1)} %get-tuple-element.26), channel_id=1, source_target_pairs={{8,0},{16,8},{24,16},{32,24},{40,32},{48,40},{56,48},{64,56},{72,6... | collective-permute-start | bytes 49160 | tf_op jit(solution)/shard_map/ppermute | solution.py:72
  174.4 1.7 collective-permute-start.7
  176.3 1.1 collective-permute-done.4
  177.4 0.2 collective-permute-done.7
  177.9 0.1 mul.174
  178.0 6.1 %fusion.12 = bf16[8,384,384]{2,1,0:T(8,128)(2,1)} fusion(bf16[1,1,8,384,512]{4,3,2,1,0:T(8,128)(2,1)} %param.8, f32[8,512]{1,0:T(8,128)S(1)} %mul.174), kind=kOutput, calls=%fused_computation.16 | convolution fusion | flops 1213857792 | bytes 5521408 | tf_op jit(solution)/shard_map/tip,tjp->tij/dot_general | solution.py:179
  184.1 5.9 %convert_element_type.43 = bf16[8,3,128,3,128]{4,3,2,1,0:T(4,128)(2,1)S(1)} reshape(bf16[8,384,384]{2,1,0:T(8,128)(2,1)} %fusion.12) | data formatting | bytes 4718592 | tf_op jit(solution)/shard_map/convert_element_type | solution.py:183
  190.0 0.7 copy.50
  190.6 4.1 convolution_convert_fusion
  194.7 7.7 %reshape.217 = bf16[64,2,16384]{2,1,0:T(2,128)(2,1)} reshape(bf16[128,16384]{1,0:T(8,128)(2,1)} %convolution_convert_fusion) | data formatting | bytes 8388608 | tf_op jit(solution)/shard_map/reshape | solution.py:188
  202.4 11.2 %all-to-all-start.2 = ((bf16[64,2,16384]{2,1,0:T(2,128)(2,1)}), bf16[64,2,16384]{2,1,0:T(2,128)(2,1)}, u32[]{:S(2)}, u32[]{:S(2)}) async-start(bf16[64,2,16384]{2,1,0:T(2,128)(2,1)} %reshape.217), calls=%async_computation.2 | async-start | bytes 8388608 | tf_op jit(solution)/shard_map/all_to_all | solution.py:187
  213.8 184.0 %all-to-all-done.2 = bf16[64,2,16384]{2,1,0:T(2,128)(2,1)} async-done(((bf16[64,2,16384]{2,1,0:T(2,128)(2,1)}), bf16[64,2,16384]{2,1,0:T(2,128)(2,1)}, u32[]{:S(2)}, u32[]{:S(2)}) %all-to-all-start.2) | async-done | bytes 4194336 | tf_op jit(solution)/shard_map/all_to_all | solution.py:187
  397.8 1.3 broadcast_in_dim.16
  399.1 11.1 %all-to-all-start.3 = ((bf16[8,2,2,128,128]{4,3,2,1,0:T(8,128)(2,1)}), bf16[8,2,2,128,128]{4,3,2,1,0:T(8,128)(2,1)S(1)}, u32[]{:S(2)}, u32[]{:S(2)}) async-start(bf16[8,2,2,128,128]{4,3,2,1,0:T(8,128)(2,1)} %broadcast_in_dim.16), calls=%async_computation.3 | async-start | bytes 2097152 | tf_op jit(solution)/shard_map/all_to_all | solution.py:85
  410.3 0.1 copy.48
  410.4 0.1 eq.58
  410.6 7.3 %reshape.218 = bf16[128,16384]{1,0:T(8,128)(2,1)} reshape(bf16[64,2,16384]{2,1,0:T(2,128)(2,1)} %all-to-all-done.2) | data formatting | bytes 8388608 | tf_op jit(solution)/shard_map/reshape | solution.py:199
  417.8 6.3 %copy.51 = bf16[128,16384]{0,1:T(8,128)(2,1)} copy(bf16[128,16384]{1,0:T(8,128)(2,1)} %reshape.218) | data formatting | bytes 8388608 | tf_op jit(solution)/shard_map/reshape | solution.py:199
  424.2 3.4 fusion.47
  427.6 3.4 collective-permute-start.8
  430.9 5.8 %collective-permute-start.9 = (bf16[2,2,128,128]{3,1,2,0:T(2,128)(2,1)S(1)}, bf16[2,2,128,128]{3,1,2,0:T(2,128)(2,1)S(1)}, u32[]{:S(2)}, u32[]{:S(2)}) collective-permute-start(bf16[2,2,128,128]{3,1,2,0:T(2,128)(2,1)S(1)} %get-tuple-element.41), channel_id=1, source_target_pairs={{8,0},{16,8},{24,16},{32,24},{40,32},{48,40},{56,48},{64,56},{72,6... | collective-permute-start | bytes 393224 | tf_op jit(solution)/shard_map/ppermute | solution.py:56
  436.8 0.1 copy.52
  436.9 0.8 gather_fusion.1
  437.7 0.7 collective-permute-done.8
  438.3 1.2 collective-permute-done.9
  439.5 0.5 pad_maximum_fusion
  440.1 0.7 gather_fusion.2
  440.9 0.4 fusion.48
  441.3 2.0 collective-permute-start.10
  443.3 7.6 %collective-permute-start.11 = (bf16[2,2,128,128]{3,2,1,0:T(8,128)(2,1)S(1)}, bf16[2,2,128,128]{3,2,1,0:T(8,128)(2,1)S(1)}, u32[]{:S(2)}, u32[]{:S(2)}) collective-permute-start(bf16[2,2,128,128]{3,2,1,0:T(8,128)(2,1)S(1)} %bitcast.112), channel_id=1, source_target_pairs={{8,0},{16,8},{24,16},{32,24},{40,32},{48,40},{56,48},{64,56},{72,6... | collective-permute-start | bytes 393224 | tf_op jit(solution)/shard_map/ppermute | solution.py:56
  451.0 0.7 copy.54
  451.7 0.3 collective-permute-done.10
  452.0 1.5 collective-permute-done.11
  453.5 0.7 gather_fusion.3
  454.3 1.1 fusion.18
  (54 shorter events, 1.4 us)
Async XLA Ops:
  7.2 124.3 %all-gather.2.cloned.1.call-start = ((), (), s32[]{:S(2)}) async-start(), calls=%async_computation.4 | async-start | bytes 8912896 | tf_op jit(solution)/shard_map/all_gather | solution.py:43
  26.1 27.8 %all-to-all-start = ((s32[16,4,1,2]{1,3,2,0:T(2,128)}), s32[16,4,1,2]{1,3,2,0:T(2,128)S(1)}, u32[]{:S(2)}, u32[]{:S(2)}) async-start(s32[16,4,1,2]{1,3,2,0:T(2,128)} %copy.46), calls=%async_computation | async-start | bytes 32768 | tf_op jit(solution)/shard_map/all_to_all | solution.py:31
  54.6 147.8 %all-to-all-start.1 = ((s32[16,4,1,2]{0,3,2,1:T(2,128)}), s32[16,4,1,2]{0,3,2,1:T(2,128)S(1)}, u32[]{:S(2)}, u32[]{:S(2)}) async-start(s32[16,4,1,2]{0,3,2,1:T(2,128)} %copy.47), calls=%async_computation.1 | async-start | bytes 8192 | tf_op jit(solution)/shard_map/all_to_all | solution.py:31
  145.3 19.4 %copy-start.1 = (f32[2,16,128]{2,1,0:T(8,128)S(1)}, f32[2,16,128]{2,1,0:T(8,128)}, u32[]{:S(2)}) copy-start(f32[2,16,128]{2,1,0:T(8,128)} %param.11) | copy-start | bytes 49156
  151.1 9.4 %collective-permute-start.1 = (f32[1,16,128]{2,1,0:T(8,128)S(1)}, f32[1,16,128]{2,1,0:T(8,128)S(1)}, u32[]{:S(2)}, u32[]{:S(2)}) collective-permute-start(f32[1,16,128]{2,1,0:T(8,128)S(1)} %slice.96), channel_id=1, source_target_pairs={{0,8},{8,16},{16,24},{24,32},{32,40},{40,48},{48,56},{56,64},{64,7... | collective-permute-start | bytes 24584 | tf_op jit(solution)/shard_map/ppermute | solution.py:54
  154.5 7.2 %collective-permute-start = (f32[1,16,128]{2,1,0:T(8,128)S(1)}, f32[1,16,128]{2,1,0:T(8,128)S(1)}, u32[]{:S(2)}, u32[]{:S(2)}) collective-permute-start(f32[1,16,128]{2,1,0:T(8,128)S(1)} %slice.93), channel_id=1, source_target_pairs={{8,0},{16,8},{24,16},{32,24},{40,32},{48,40},{56,48},{64,56},{72,6... | collective-permute-start | bytes 24584 | tf_op jit(solution)/shard_map/ppermute | solution.py:56
  161.7 1.3 collective-permute-start.2
  161.7 3.0 collective-permute-start.3
  164.9 12.7 %collective-permute-start.5 = (f32[2,1,16,128]{3,2,1,0:T(8,128)S(1)}, f32[2,1,16,128]{3,2,1,0:T(8,128)S(1)}, u32[]{:S(2)}, u32[]{:S(2)}) collective-permute-start(f32[2,1,16,128]{3,2,1,0:T(8,128)S(1)} %get-tuple-element.25), channel_id=1, source_target_pairs={{0,8},{8,16},{16,24},{24,32},{32,40},{40,48},{48,56},{56,64},{64,7... | collective-permute-start | bytes 49160 | tf_op jit(solution)/shard_map/ppermute | solution.py:71
  166.8 10.8 %collective-permute-start.6 = (f32[2,1,16,128]{3,2,1,0:T(8,128)S(1)}, f32[2,1,16,128]{3,2,1,0:T(8,128)S(1)}, u32[]{:S(2)}, u32[]{:S(2)}) collective-permute-start(f32[2,1,16,128]{3,2,1,0:T(8,128)S(1)} %get-tuple-element.26), channel_id=1, source_target_pairs={{8,0},{16,8},{24,16},{32,24},{40,32},{48,40},{56,48},{64,56},{72,6... | collective-permute-start | bytes 49160 | tf_op jit(solution)/shard_map/ppermute | solution.py:72
  174.3 3.0 collective-permute-start.4
  174.4 3.2 collective-permute-start.7
  177.7 6.3 %copy-start.2 = (f32[2,16,128]{2,1,0:T(8,128)}, f32[2,16,128]{2,1,0:T(8,128)S(1)}, u32[]{:S(2)}) copy-start(f32[2,16,128]{2,1,0:T(8,128)S(1)} %fusion.26) | copy-start | bytes 49156
  202.4 11.2 %copy-start.3 = (s32[2,2,8]{2,1,0:T(2,128)S(1)}, s32[2,2,8]{2,1,0:T(2,128)}, u32[]{:S(2)}) copy-start(s32[2,2,8]{2,1,0:T(2,128)} %param.15) | copy-start | bytes 388
  202.4 11.3 %copy-start.4 = (s32[2,2,8]{2,1,0:T(2,128)S(1)}, s32[2,2,8]{2,1,0:T(2,128)}, u32[]{:S(2)}) copy-start(s32[2,2,8]{2,1,0:T(2,128)} %param.14) | copy-start | bytes 388
  202.4 195.4 %copy-start = (bf16[2,2,128,128]{3,2,1,0:T(8,128)(2,1)S(1)}, bf16[2,2,128,128]{3,2,1,0:T(8,128)(2,1)}, u32[]{:S(2)}) copy-start(bf16[2,2,128,128]{3,2,1,0:T(8,128)(2,1)} %param.10) | copy-start | bytes 393220
  202.4 195.4 %all-to-all-start.2 = ((bf16[64,2,16384]{2,1,0:T(2,128)(2,1)}), bf16[64,2,16384]{2,1,0:T(2,128)(2,1)}, u32[]{:S(2)}, u32[]{:S(2)}) async-start(bf16[64,2,16384]{2,1,0:T(2,128)(2,1)} %reshape.217), calls=%async_computation.2 | async-start | bytes 8388608 | tf_op jit(solution)/shard_map/all_to_all | solution.py:187
  399.1 37.7 %all-to-all-start.3 = ((bf16[8,2,2,128,128]{4,3,2,1,0:T(8,128)(2,1)}), bf16[8,2,2,128,128]{4,3,2,1,0:T(8,128)(2,1)S(1)}, u32[]{:S(2)}, u32[]{:S(2)}) async-start(bf16[8,2,2,128,128]{4,3,2,1,0:T(8,128)(2,1)} %broadcast_in_dim.16), calls=%async_computation.3 | async-start | bytes 2097152 | tf_op jit(solution)/shard_map/all_to_all | solution.py:85
  427.6 10.8 %collective-permute-start.8 = (bf16[2,2,128,128]{3,1,2,0:T(2,128)(2,1)S(1)}, bf16[2,2,128,128]{3,1,2,0:T(2,128)(2,1)S(1)}, u32[]{:S(2)}, u32[]{:S(2)}) collective-permute-start(bf16[2,2,128,128]{3,1,2,0:T(2,128)(2,1)S(1)} %get-tuple-element.41), channel_id=1, source_target_pairs={{0,8},{8,16},{16,24},{24,32},{32,40},{40,48},{48,56},{56,64},{64,7... | collective-permute-start | bytes 393224 | tf_op jit(solution)/shard_map/ppermute | solution.py:54
  430.9 8.6 %collective-permute-start.9 = (bf16[2,2,128,128]{3,1,2,0:T(2,128)(2,1)S(1)}, bf16[2,2,128,128]{3,1,2,0:T(2,128)(2,1)S(1)}, u32[]{:S(2)}, u32[]{:S(2)}) collective-permute-start(bf16[2,2,128,128]{3,1,2,0:T(2,128)(2,1)S(1)} %get-tuple-element.41), channel_id=1, source_target_pairs={{8,0},{16,8},{24,16},{32,24},{40,32},{48,40},{56,48},{64,56},{72,6... | collective-permute-start | bytes 393224 | tf_op jit(solution)/shard_map/ppermute | solution.py:56
  441.3 10.6 %collective-permute-start.10 = (bf16[2,2,128,128]{3,2,1,0:T(8,128)(2,1)S(1)}, bf16[2,2,128,128]{3,2,1,0:T(8,128)(2,1)S(1)}, u32[]{:S(2)}, u32[]{:S(2)}) collective-permute-start(bf16[2,2,128,128]{3,2,1,0:T(8,128)(2,1)S(1)} %bitcast.111), channel_id=1, source_target_pairs={{0,8},{8,16},{16,24},{24,32},{32,40},{40,48},{48,56},{56,64},{64,7... | collective-permute-start | bytes 393224 | tf_op jit(solution)/shard_map/ppermute | solution.py:54
  443.3 10.2 %collective-permute-start.11 = (bf16[2,2,128,128]{3,2,1,0:T(8,128)(2,1)S(1)}, bf16[2,2,128,128]{3,2,1,0:T(8,128)(2,1)S(1)}, u32[]{:S(2)}, u32[]{:S(2)}) collective-permute-start(bf16[2,2,128,128]{3,2,1,0:T(8,128)(2,1)S(1)} %bitcast.112), channel_id=1, source_target_pairs={{8,0},{16,8},{24,16},{32,24},{40,32},{48,40},{56,48},{64,56},{72,6... | collective-permute-start | bytes 393224 | tf_op jit(solution)/shard_map/ppermute | solution.py:56
Sparse Core Ops, SparseCore 0:
  22.1 109.2 all-gather.1
where the time goes:
time: 464 us; the launch traced here: 462 us
  waiting for transfers between devices  278 us (60%)
  starting transfers between devices  80.5 us (17%)
  local copies, waits for them, and re-layouts  49.2 us (11%)
  matrix products  20.5 us (4%)
  blocking collectives  14.8 us (3%)
  between operations  14.4 us (3%)
  other arithmetic  4.72 us (1%)
    all_to_all x1, waiting for transfers between devices, body(): lax.all_to_all(outgoing_parts.reshape(slab_count, capacity, block_width *...  184 us
    all_gather x1, waiting for transfers between devices, gathered_by_axis(): result = lax.all_gather(result, axes[number], axis=dim, tiled=True)  73.6 us
    ppermute x4, starting transfers between devices, padded_2(): lax.ppermute(head, axis, [((i + 1) % count, i) for i in range(count)])  19.3 us
    all_to_all x2, starting transfers between devices, turned_blocks(): lax.all_to_all(blocks, axes[k], split_axis=k, concat_axis=k, tiled=True)  18.4 us
    all_gather x1, blocking collectives, gathered_by_axis(): result = lax.all_gather(result, axes[number], axis=dim, tiled=True)  14.8 us
    reshape x2, local copies, waits for them, and re-layouts, body(): returned.reshape(slab_count * capacity, block_width * block_width)  13.6 us
    all_to_all x2, waiting for transfers between devices, turned_blocks(): lax.all_to_all(blocks, axes[k], split_axis=k, concat_axis=k, tiled=True)  11.9 us
    all_to_all x1, starting transfers between devices, body(): lax.all_to_all(outgoing_parts.reshape(slab_count, capacity, block_width *...  11.2 us
  transfers between devices with their start and end apart: 17, of which 12 were waited for; matrix products, arithmetic and copies ran while one was open for 15% of the time, Pallas kernels for 0%

commit v1 on v0

v1 whole, which is shorter than its diff:
```python
import functools
import math

import jax
import jax.numpy as jnp
from jax import lax
from jax.experimental import pallas as pl
from jax.experimental.pallas import tpu as pltpu
from jax.sharding import PartitionSpec as P

MESH = pl.DeviceIdType.MESH
NX = 4
SPACING = 0.1
KAPPA = 0.804
MU = 0.2195
FERMI_SQ = (3.0 * math.pi**2) ** (2.0 / 3.0)
AMPLITUDE = 0.75 * (3.0 / math.pi) ** (1.0 / 3.0)
ROWS = 32


def place_arrays(owners, sources, depth):
    me = lax.axis_index("wide")
    pairs = owners.shape[0]
    order = jnp.arange(pairs, dtype=jnp.int32)
    dz = jnp.mod(owners // NX - me // NX, depth)
    dx = jnp.mod(owners % NX - me % NX, NX)
    same = (owners[:, None] == owners[None, :]) & (order[None, :] < order[:, None])
    seat = jnp.sum(same.astype(jnp.int32), axis=1)
    slot = dx * (2 * depth) + dz * 2 + seat
    slots = jnp.arange(2 * NX * depth, dtype=jnp.int32)
    hit = slot[:, None] == slots[None, :]
    slot_pair = jnp.sum(jnp.where(hit, order[:, None] - pairs, 0), axis=0) + pairs
    slot_source = jnp.sum(jnp.where(hit, sources[:, None] + 1, 0), axis=0) - 1
    entry = jnp.where(
        dx == 0,
        dz * 4 + sources,
        jnp.where(
            dx == 3,
            4 * depth + dz * 3 + seat,
            jnp.where(dx == 1, 7 * depth + dz * 3 + seat, 10 * depth + seat * depth + dz),
        ),
    )
    return slot_pair, slot_source, entry


def step_kernel(
    depth,
    slot_pair,
    entry,
    left_at,
    right_at,
    req,
    dens,
    lnv,
    core,
    phi_hbm,
    pot_out,
    ham_out,
    grad_out,
    phi,
    want,
    buf,
    xsend,
    parts,
    rsend,
    rleft,
    rright,
    rfleft,
    rfright,
    zin,
    zout,
    lnv_all,
    lnv_cat,
    tile_matrix,
    charge,
    halo,
    flux,
    halo2,
    window,
    window2,
    ham_half,
    first_half,
    phi_sem,
    want_sem,
    lnv_sem,
    z_sem,
    x_sem,
    f_sem,
    rx_sem,
    rf_sem,
    rz_sem,
    halo_sem,
    win_sem,
):
    w = lax.axis_index("wide")
    c = lax.axis_index("col")
    wides = depth * NX
    cols = lax.axis_size("col")
    tiles = charge.shape[0]
    half = depth // 2
    ob = dens.shape[1]
    z, x = lax.div(w, NX), lax.rem(w, NX)

    def chip(dz, dx):
        return (lax.rem(z + depth + dz, depth) * NX + lax.rem(x + NX + dx, NX), c)

    zup, zdn, xr, xl, x2 = chip(1, 0), chip(-1, 0), chip(0, 1), chip(0, -1), chip(0, 2)
    wp = (lax.rem(w + 1, wides), c)
    wm = (lax.rem(w + wides - 1, wides), c)
    strip = [(w, lax.rem(c + d, cols)) for d in range(1, cols)]
    cp, cm = strip[0], strip[-1]

    def remote(src, dst, sems, index, device):
        return pltpu.make_async_remote_copy(
            src_ref=src,
            dst_ref=dst,
            send_sem=sems.at[(0, *index)],
            recv_sem=sems.at[(1, *index)],
            device_id=device,
            device_id_type=MESH,
        )

    phi_copy = pltpu.make_async_copy(phi_hbm, phi, phi_sem)
    phi_copy.start()

    barrier = pltpu.get_barrier_semaphore()
    greeted = [zup, zdn, xr, xl, x2, wp, wm, *strip]
    for device in greeted:
        pl.semaphore_signal(barrier, inc=1, device_id=device, device_id_type=MESH)
    pl.semaphore_wait(barrier, len(greeted))

    left0, right0, fleft0, fright0 = 4 * depth, 7 * depth, 10 * depth, 11 * depth
    span = 2 * depth

    def z_copy(k, way, lo=0, hi=4):
        if way == 0:
            j = lax.rem(depth - k, depth)
            return remote(
                buf.at[pl.ds(4 * j + lo, hi - lo)],
                buf.at[pl.ds(4 * (depth - k - 1) + lo, hi - lo)],
                z_sem, (0, k), zup,
            )
        return remote(
            buf.at[pl.ds(4 * k + lo, hi - lo)], buf.at[pl.ds(4 * k + 4 + lo, hi - lo)], z_sem, (1, k), zdn
        )

    def x_copy(j, way):
        if way == 0:
            return remote(xsend.at[0, j], buf.at[pl.ds(left0 + 3 * j, 3)], x_sem, (0, j), xr)
        return remote(xsend.at[1, j], buf.at[pl.ds(right0 + 3 * j, 3)], x_sem, (1, j), xl)

    def f_copy(j, way):
        if way == 0:
            return remote(buf.at[left0 + 3 * j + 2], buf.at[fleft0 + j], f_sem, (0, j), xr)
        return remote(buf.at[right0 + 3 * j + 2], buf.at[fright0 + j], f_sem, (1, j), xl)

    def pack(j):
        wanted = (((3, 0), (3, 1), (2, 0)), ((1, 0), (1, 1), (2, 1)))
        for lo in range(0, ob, ROWS):
            rows = pl.ds(lo, ROWS)
            b = [buf[4 * j + s, rows, :].astype(jnp.float32) for s in range(4)]
            for way in range(2):
                for n, (dx, seat) in enumerate(wanted[way]):
                    src = want[pl.ds(dx * span + 2 * j + seat, 1), :]
                    got = jnp.where(
                        src == 0, b[0], jnp.where(src == 1, b[1], jnp.where(src == 2, b[2], b[3]))
                    )
                    xsend[way, j, n, rows, :] = got.astype(jnp.bfloat16)
        for way in range(2):
            x_copy(j, way).start()

    def forward(j):
        for way in range(2):
            x_copy(j, way).wait_recv()
            f_copy(j, way).start()

    def want_copy(dx, device):
        rows = pl.ds(dx * span, span)
        return remote(req.at[rows], want.at[rows], want_sem, (dx,), device)

    for s in range(4):
        buf[s] = dens[s]
    want_copies = [want_copy(1, xr), want_copy(3, xl), want_copy(2, x2)]
    for copy in want_copies:
        copy.start()
    for way in range(2):
        z_copy(0, way).start()

    def lnv_copy(d):
        return remote(lnv, lnv_all.at[pl.ds(4 * (cols - d), 4)], lnv_sem, (d,), strip[d - 1])

    for d in range(1, cols):
        lnv_copy(d).start()
    for s in range(4):
        lnv_all[s] = lnv[s]
    want[pl.ds(0, span), :] = req[pl.ds(0, span), :]
    for copy in want_copies:
        copy.wait_recv()
    pack(0)

    def gather_step(k, carry):
        for way in range(2):
            z_copy(k - 1, way).wait_recv()
            z_copy(k, way).start()
        pack(depth - k)
        pack(k)

        @pl.when(k == 2)
        def _():
            forward(0)

        @pl.when(k > 2)
        def _():
            forward(depth - k + 2)
            forward(k - 2)

        return carry

    lax.fori_loop(1, half - 1, gather_step, 0)
    for way in range(2):
        z_copy(half - 2, way).wait_recv()
        z_copy(half - 1, way, 2 * way, 2 * way + 2).start()
    pack(half + 1)
    pack(half - 1)
    for k in range(half - 3, half - 1):
        if k == 0:
            forward(0)
        elif k > 0:
            forward(depth - k)
            forward(k)
    for way in range(2):
        z_copy(half - 1, way, 2 * way, 2 * way + 2).wait_recv()
    pack(half)
    forward(half + 1)
    forward(half - 1)
    forward(half)

    def gather_end(j, carry):
        for way in range(2):
            f_copy(j, way).wait_recv()
        return carry

    lax.fori_loop(0, depth, gather_end, 0)
    phi_copy.wait()

    def charge_step(t, carry):
        for a in range(3):
            for b in range(3):
                tile_matrix[pl.ds(ob * a, ob), pl.ds(ob * b, ob)] = buf[entry[9 * t + 3 * a + b]]
        values = phi[t]
        applied = jnp.dot(tile_matrix[...], values, preferred_element_type=jnp.float32)
        charge[pl.ds(t, 1), :] = jnp.sum(values.astype(jnp.float32) * applied, axis=0, keepdims=True)
        return carry

    lax.fori_loop(0, tiles, charge_step, 0)

    sides = (wp, wm, cp, cm)

    def halo_copy(src, dst, first, n):
        return remote(src, dst.at[n], halo_sem, (first + n,), sides[n])

    for n in range(4):
        halo_copy(charge, halo, 0, n).start()

    points = charge.shape[1]
    xcell, ycell, zcell = points // 2, points // 32, 1
    lane = lax.broadcasted_iota(jnp.int32, (tiles, points), 1)
    at_x = lax.div(lane, xcell)
    at_y = lax.rem(lax.div(lane, ycell), 16)
    at_z = lax.rem(lane, 16)

    def turned(a, shift):
        return pltpu.roll(a, shift % points, 1)

    def x_next(a, beyond):
        return turned(jnp.where(at_x == 1, a, beyond), xcell)

    def x_prev(a, beyond):
        return turned(jnp.where(at_x == 0, a, beyond), xcell)

    def y_next(a, beyond):
        return jnp.where(at_y < 15, turned(a, -ycell), turned(beyond, 15 * ycell))

    def y_prev(a, beyond):
        return jnp.where(at_y > 0, turned(a, ycell), turned(beyond, -15 * ycell))

    def z_next(a):
        return jnp.where(at_z < 15, turned(a, -1), turned(pltpu.roll(a, tiles - 1, 0), 15))

    def z_prev(a):
        return jnp.where(at_z > 0, turned(a, 1), turned(pltpu.roll(a, 1, 0), -15))

    rho = charge[...]
    for n in range(4):
        halo_copy(charge, halo, 0, n).wait_recv()
    grad_x = (x_next(rho, halo[1]) - x_prev(rho, halo[0])) / (2.0 * SPACING)
    grad_y = (y_next(rho, halo[3]) - y_prev(rho, halo[2])) / (2.0 * SPACING)
    grad_z = (z_next(rho) - z_prev(rho)) / (2.0 * SPACING)
    sigma = grad_x * grad_x + grad_y * grad_y + grad_z * grad_z
    n_sq = rho * rho + core[...] * core[...]
    third = jnp.exp(jnp.log(n_sq) * (1.0 / 6.0))
    smooth = jnp.sqrt(n_sq)
    four_thirds = smooth * third
    s2 = sigma / (4.0 * FERMI_SQ * four_thirds * four_thirds)
    denom = 1.0 + MU * s2 / KAPPA
    enhance = 1.0 + KAPPA - KAPPA / denom
    slope = MU / (denom * denom)
    de_dn = -AMPLITUDE * third * ((4.0 / 3.0) * enhance - (8.0 / 3.0) * s2 * slope)
    de_dsigma = -AMPLITUDE * slope / (4.0 * FERMI_SQ * four_thirds)
    flux_x = 2.0 * de_dsigma * grad_x
    flux_y = 2.0 * de_dsigma * grad_y
    flux_z = 2.0 * de_dsigma * grad_z
    flux[0] = flux_x
    flux[1] = flux_y
    for n in range(4):
        halo_copy(flux.at[n // 2], halo2, 4, n).start()
    partial = de_dn * rho / smooth + (z_prev(flux_z) - z_next(flux_z)) / (2.0 * SPACING)
    for n in range(4):
        halo_copy(flux.at[n // 2], halo2, 4, n).wait_recv()
    divergence = (
        x_prev(flux_x, halo2[0])
        - x_next(flux_x, halo2[1])
        + y_prev(flux_y, halo2[2])
        - y_next(flux_y, halo2[3])
    )
    pot_out[...] = partial + divergence / (2.0 * SPACING)

    parts[9 * tiles] = jnp.zeros((ob, ob), jnp.bfloat16)

    def part_step(t, carry):
        values = phi[t]
        weighted = (values.astype(jnp.float32) * pot_out[pl.ds(t, 1), :]).astype(jnp.bfloat16)
        block = lax.dot_general(
            weighted, values, (((1,), (1,)), ((), ())), preferred_element_type=jnp.float32
        ).astype(jnp.bfloat16)
        for a in range(3):
            for b in range(3):
                parts[9 * t + 3 * a + b] = block[ob * a : ob * a + ob, ob * b : ob * b + ob]
        return carry

    lax.fori_loop(0, tiles, part_step, 0)

    def rx_copy(j, way):
        return remote(rsend.at[way, j], (rleft, rright)[way].at[j], rx_sem, (way, j), (xr, xl)[way])

    def rf_copy(j, way):
        return remote(
            (rleft, rright)[way].at[j, 2], (rfleft, rfright)[way].at[j], rf_sem, (way, j), (xr, xl)[way]
        )

    def rz_copy(k, way, lo=0, hi=4):
        rows = pl.ds(lo, hi - lo)
        return remote(zout.at[way, k, rows], zin.at[way, k, rows], rz_sem, (way, k), (zup, zdn)[way])

    def give(j):
        slots = (((1, 0), (1, 1), (2, 0)), ((3, 0), (3, 1), (2, 1)))
        for way in range(2):
            for n, (dx, seat) in enumerate(slots[way]):
                rsend[way, j, n] = parts[slot_pair[dx * span + 2 * j + seat]]
            rx_copy(j, way).start()

    def pass_on(j):
        for way in range(2):
            rx_copy(j, way).wait_recv()
            rf_copy(j, way).start()

    def summed(j, lo):
        rows = pl.ds(lo, ROWS)
        pieces = [
            (0, 0, parts[slot_pair[2 * j], rows, :]),
            (0, 1, parts[slot_pair[2 * j + 1], rows, :]),
            (1, 0, rleft[j, 0, rows, :]),
            (1, 1, rleft[j, 1, rows, :]),
            (3, 0, rright[j, 0, rows, :]),
            (3, 1, rright[j, 1, rows, :]),
            (2, 0, rfleft[j, rows, :]),
            (2, 1, rfright[j, rows, :]),
        ]
        total = [jnp.zeros((ROWS, ob), jnp.float32)] * 4
        for dx, seat, piece in pieces:
            src = want[pl.ds(dx * span + 2 * j + seat, 1), :]
            piece = piece.astype(jnp.float32)
            total = [t + jnp.where(src == s, piece, 0.0) for s, t in enumerate(total)]
        return total

    def arrived(j):
        for way in range(2):
            rf_copy(j, way).wait_recv()

    for s in range(2):
        zin[0, 0, 2 + s] = jnp.zeros((ob, ob), jnp.bfloat16)
        zin[1, 0, s] = jnp.zeros((ob, ob), jnp.bfloat16)
    give(half)
    give(half - 1)
    give(half + 1)
    pass_on(half)
    give(half - 2)
    give(half + 2)
    pass_on(half - 1)
    pass_on(half + 1)
    arrived(half)
    for lo in range(0, ob, ROWS):
        total = summed(half, lo)
        for s in range(4):
            zout[s // 2, 0, s, pl.ds(lo, ROWS), :] = total[s].astype(jnp.bfloat16)
    for way in range(2):
        rz_copy(0, way, 2 * way, 2 * way + 2).start()

    def reduce_step(k, carry):
        @pl.when(k < half - 2)
        def _():
            give(half - k - 2)
            give(half + k + 2)

        @pl.when(k == half - 2)
        def _():
            give(0)

        @pl.when(k < half - 1)
        def _():
            pass_on(half - k - 1)
            pass_on(half + k + 1)

        @pl.when(k == half - 1)
        def _():
            pass_on(0)

        for way in range(2):
            j = half - k if way == 0 else half + k
            arrived(j)

            @pl.when(k == 1)
            def _():
                rz_copy(0, way, 2 * way, 2 * way + 2).wait_recv()

            @pl.when(k > 1)
            def _():
                rz_copy(k - 1, way).wait_recv()

            for lo in range(0, ob, ROWS):
                rows = pl.ds(lo, ROWS)
                total = summed(j, lo)
                for s in range(4):
                    zout[way, k, s, rows, :] = (
                        total[s] + zin[way, k - 1, s, rows, :].astype(jnp.float32)
                    ).astype(jnp.bfloat16)
            rz_copy(k, way).start()
        return carry

    lax.fori_loop(1, half, reduce_step, 0)

    for d in range(1, cols):
        lnv_copy(d).wait_recv()

    def left_step(n, carry):
        for t in range(8):
            lnv_cat[n, :, pl.ds(ob * t, ob)] = lnv_all[left_at[8 * n + t]]
        return carry

    lax.fori_loop(0, 4, left_step, 0)
    arrived(0)
    for way in range(2):
        rz_copy(half - 1, way).wait_recv()
    for lo in range(0, ob, ROWS):
        rows = pl.ds(lo, ROWS)
        total = summed(0, lo)
        for s in range(4):
            value = (
                total[s]
                + zin[0, half - 1, s, rows, :].astype(jnp.float32)
                + zin[1, half - 1, s, rows, :].astype(jnp.float32)
            )
            ham_out[s, rows, :] = value
            ham_half[s, rows, :] = value.astype(jnp.bfloat16)

    def win_copy(src, dst, first, n):
        return remote(src, dst.at[pl.ds(8 * n, 4)], win_sem, (first + n,), (wp, wm)[n])

    def product(n, win):
        chosen = jnp.concatenate([win[right_at[8 * n + t]] for t in range(8)], axis=0)
        return jnp.dot(lnv_cat[n], chosen, preferred_element_type=jnp.float32)

    for n in range(2):
        win_copy(ham_half, window, 0, n).start()
    for s in range(4):
        window[4 + s] = ham_half[s]
    for n in range(2):
        win_copy(ham_half, window, 0, n).wait_recv()
    for n in range(4):
        first = product(n, window)
        grad_out[n] = first
        first_half[n] = first.astype(jnp.bfloat16)
    for n in range(2):
        win_copy(first_half, window2, 2, n).start()
    for s in range(4):
        window2[4 + s] = first_half[s]
    for n in range(2):
        win_copy(first_half, window2, 2, n).wait_recv()
    for n in range(4):
        grad_out[n] = 3.0 * grad_out[n] - 2.0 * product(n, window2)

    for copy in want_copies:
        copy.wait_send()
    for d in range(1, cols):
        lnv_copy(d).wait_send()
    for n in range(4):
        halo_copy(charge, halo, 0, n).wait_send()
        halo_copy(flux.at[n // 2], halo2, 4, n).wait_send()
    for n in range(2):
        win_copy(ham_half, window, 0, n).wait_send()
        win_copy(first_half, window2, 2, n).wait_send()
    for way in range(2):
        z_copy(half - 1, way, 2 * way, 2 * way + 2).wait_send()
        rz_copy(0, way, 2 * way, 2 * way + 2).wait_send()

    def sent_x(j, carry):
        for way in range(2):
            x_copy(j, way).wait_send()
            f_copy(j, way).wait_send()
            rx_copy(j, way).wait_send()
            rf_copy(j, way).wait_send()
        return carry

    def sent_z(k, carry):
        for way in range(2):
            z_copy(k, way).wait_send()
            rz_copy(k + 1, way).wait_send()
        return carry

    lax.fori_loop(0, depth, sent_x, 0)
    lax.fori_loop(0, half - 1, sent_z, 0)


def body(phi_values, density, lnv_matrix, core_density, pair_owner, pair_source, term_left, term_right):
    phi = phi_values[0, 0]
    tiles, _, points = phi.shape
    ob = density.shape[-1]
    depth = lax.axis_size("wide") // NX
    cols = lax.axis_size("col")
    half = depth // 2
    slot_pair, slot_source, entry = place_arrays(pair_owner[0, 0, :, 0], pair_source[0, 0], depth)
    req = jnp.broadcast_to(slot_source[:, None], (2 * NX * depth, ob))
    row = jnp.arange(2, dtype=jnp.int32)[:, None, None]
    left_at = jnp.mod(term_left // 2 - lax.axis_index("col"), cols) * 4 + row * 2 + term_left % 2
    slabs, strips, deep = core_density.shape
    core = (
        core_density.reshape(slabs, strips, tiles, deep // tiles).transpose(2, 0, 1, 3).reshape(tiles, points)
    )
    block = lambda *n: pltpu.VMEM((*n, ob, ob), jnp.bfloat16)
    sems = lambda *n: pltpu.SemaphoreType.DMA((2, *n))
    vmem = pl.BlockSpec(memory_space=pltpu.VMEM)
    smem = pl.BlockSpec(memory_space=pltpu.SMEM)
    pot, ham, grad = pl.pallas_call(
        functools.partial(step_kernel, depth),
        out_shape=(
            jax.ShapeDtypeStruct((tiles, points), jnp.float32),
            jax.ShapeDtypeStruct((4, ob, ob), jnp.float32),
            jax.ShapeDtypeStruct((4, ob, ob), jnp.float32),
        ),
        in_specs=[smem] * 4 + [vmem] * 4 + [pl.BlockSpec(memory_space=pl.ANY)],
        out_specs=(vmem, vmem, vmem),
        scratch_shapes=[
            pltpu.VMEM(phi.shape, jnp.bfloat16),
            pltpu.VMEM(req.shape, jnp.int32),
            block(12 * depth),
            block(2, depth, 3),
            block(9 * tiles + 1),
            block(2, depth, 3),
            block(depth, 3),
            block(depth, 3),
            block(depth),
            block(depth),
            block(2, half, 4),
            block(2, half, 4),
            block(4 * cols),
            pltpu.VMEM((4, ob, 8 * ob), jnp.bfloat16),
            pltpu.VMEM((3 * ob, 3 * ob), jnp.bfloat16),
            pltpu.VMEM((tiles, points), jnp.float32),
            pltpu.VMEM((4, tiles, points), jnp.float32),
            pltpu.VMEM((2, tiles, points), jnp.float32),
            pltpu.VMEM((4, tiles, points), jnp.float32),
            block(12),
            block(12),
            block(4),
            block(4),
            pltpu.SemaphoreType.DMA,
            sems(4),
            sems(cols),
            sems(2, half),
            sems(2, depth),
            sems(2, depth),
            sems(2, depth),
            sems(2, depth),
            sems(2, half),
            sems(8),
            sems(4),
        ],
        compiler_params=pltpu.CompilerParams(
            collective_id=0, has_side_effects=True, vmem_limit_bytes=48 * 1024 * 1024
        ),
    )(
        slot_pair,
        entry,
        left_at.reshape(-1),
        term_right.reshape(-1),
        req,
        density.reshape(4, ob, ob),
        lnv_matrix.reshape(4, ob, ob),
        core,
        phi,
    )
    potential = (
        pot.reshape(tiles, slabs, strips, deep // tiles).transpose(1, 2, 0, 3).reshape(slabs, strips, deep)
    )
    return potential, ham.reshape(density.shape), grad.reshape(density.shape)


def solution(mesh):
    grid = lambda n: P("wide", "col", *([None] * n))
    return jax.shard_map(
        body,
        mesh=mesh,
        in_specs=(grid(3), grid(2), grid(2), grid(1), grid(2), grid(1), grid(1), grid(1)),
        out_specs=(grid(1), grid(2), grid(2)),
        check_vma=False,
    )
```

time: 464 us -> 162 us (0.35)
  waiting for transfers between devices: 278 us -> 0 us
  Pallas kernels: 0 us -> 150 us
  starting transfers between devices: 80.5 us -> 0 us
  local copies, waits for them, and re-layouts: 49.2 us -> 7.86 us
  matrix products: 20.5 us -> 0 us
  blocking collectives: 14.8 us -> 0 us
  between operations: 14.4 us -> 0.73 us
    all_to_all x4 -> x0, waiting for transfers between devices: 196 us -> none  [the longest x1 184 us: body(): lax.all_to_all(outgoing_parts.reshape(slab_count, capacity, block_width *...]
    pallas_call x0 -> x1, Pallas kernels: none -> 150 us  [body(): pl.pallas_call(functools.partial(step_kernel, depth), out_shape=(jax.Shap...]
    all_gather x1 -> x0, waiting for transfers between devices: 73.6 us -> none  [gathered_by_axis(): result = lax.all_gather(result, axes[number], axis=dim, tiled=True)]
    all_to_all x4 -> x0, starting transfers between devices: 40.8 us -> none  [the longest x2 18.4 us: turned_blocks(): lax.all_to_all(blocks, axes[k], split_axis=k, concat_axis=k, tiled=True)]
    ppermute x12 -> x0, starting transfers between devices: 39.7 us -> none  [the longest x4 19.3 us: padded_2(): lax.ppermute(head, axis, [((i + 1) % count, i) for i in range(count)])]
    reshape x9 -> x7, local copies, waits for them, and re-layouts: 25.9 us -> 2.61 us  [the longest x3 0.96 us: body(): core_density.reshape(slabs, strips, tiles, deep // tiles)]
    dot_general x6 -> x0, matrix products: 20.5 us -> none  [the longest x1 6.08 us: body(): jnp.einsum('tip,tjp->tij', weighted, orbital_values, preferred_element_ty...]
    all_gather x1 -> x0, blocking collectives: 14.8 us -> none  [gathered_by_axis(): result = lax.all_gather(result, axes[number], axis=dim, tiled=True)]
  transfers between devices with their start and end apart: 17 -> 0, of which waited for: 12 -> 0; matrix products, arithmetic and copies ran while one was open for 15% -> 0% of each run, Pallas kernels for 0% -> 0%
where the time goes in v1:
time: 162 us; the launch traced here: 161 us
  Pallas kernels  150 us (93%)
  local copies, waits for them, and re-layouts  7.86 us (5%)
  other arithmetic  2.49 us (2%)
    pallas_call x1, Pallas kernels, body(): pl.pallas_call(functools.partial(step_kernel, depth), out_shape=(jax.Shap...  150 us
    unnamed x8, local copies, waits for them, and re-layouts  5.09 us

profile of v1, /device:TPU:24, one launch (start us, length us, event | category | flops | bytes accessed | tf_op | source)
XLA Modules:
  0.0 161.4 jit_solution(16534034171581838402)
XLA Ops:
  0.7 0.9 convert_reduce_fusion
  1.6 0.8 reshape.137.right_at
  2.3 0.8 fusion.3
  3.1 0.1 reshape.136.left_at
  3.2 0.7 compare_select_fusion.8
  3.9 0.1 select_reduce_fusion
  4.0 0.1 broadcast_in_dim.33.req
  4.1 0.8 reshape.140
  5.0 0.1 reshape.141.core
  5.1 0.0 copy-start
  5.1 1.9 %copy-done = bf16[1,1,8,384,512]{4,3,2,1,0:T(8,128)(2,1)S(1)} copy-done((bf16[1,1,8,384,512]{4,3,2,1,0:T(8,128)(2,1)S(1)}, bf16[1,1,8,384,512]{4,3,2,1,0:T(8,128)(2,1)}, u32[]{:S(2)}) %copy-start) | copy-done | bytes 3145752
  7.0 0.0 copy-start.1
  7.0 0.9 copy-done.1
  7.9 0.0 copy-start.2
  7.9 0.9 copy-done.2
  8.8 150.3 %shard_map.103 = (f32[8,512]{1,0:T(8,128)S(1)}, f32[4,128,128]{2,1,0:T(8,128)S(1)}, f32[4,128,128]{2,1,0:T(8,128)S(1)}) custom-call(s32[128]{0:T(128)S(1)} %get-tuple-element.16.slot_pair, s32[72]{0:T(128)S(1)} %get-tuple-element.11.entry, s32[32]{0:T(128)S(1)} %reshape.136.left_at, s32[32]{0:T(128)S(1)} %reshape.137.right_at, ...), custom_call_target="tpu_custom_call" | custom-call | tf_op jit(solution)/shard_map/pallas_call | solution.py:553
  159.1 0.1 reshape.142
  159.2 0.1 copy.14
  159.3 0.7 reshape.143
  160.0 0.7 copy.19
  160.7 0.7 copy.20
  (5 shorter events, 0.0 us)
Async XLA Ops:
  5.1 1.9 %copy-start = (bf16[1,1,8,384,512]{4,3,2,1,0:T(8,128)(2,1)S(1)}, bf16[1,1,8,384,512]{4,3,2,1,0:T(8,128)(2,1)}, u32[]{:S(2)}) copy-start(bf16[1,1,8,384,512]{4,3,2,1,0:T(8,128)(2,1)} %param.8) | copy-start | bytes 9437188
  7.0 0.9 copy-start.1
  7.9 0.9 copy-start.2

commit v2 on v1

--- a/solution.py
+++ b/solution.py
@@ -31,15 +31,15 @@
     hit = slot[:, None] == slots[None, :]
     slot_pair = jnp.sum(jnp.where(hit, order[:, None] - pairs, 0), axis=0) + pairs
     slot_source = jnp.sum(jnp.where(hit, sources[:, None] + 1, 0), axis=0) - 1
+    part = jnp.arange(2, dtype=jnp.int32)[None, :]
+    dz, dx, seat, sources = dz[:, None], dx[:, None], seat[:, None], sources[:, None]
+    near = dz * 5 + seat * 2 + part
+    far = jnp.where(part == 0, 20 * depth + dz * 4 + sources, 18 * depth + seat * depth + dz)
     entry = jnp.where(
         dx == 0,
-        dz * 4 + sources,
-        jnp.where(
-            dx == 3,
-            4 * depth + dz * 3 + seat,
-            jnp.where(dx == 1, 7 * depth + dz * 3 + seat, 10 * depth + seat * depth + dz),
-        ),
-    )
+        dz * 8 + part * 4 + sources,
+        jnp.where(dx == 3, 8 * depth + near, jnp.where(dx == 1, 13 * depth + near, far)),
+    ).reshape(-1)
     return slot_pair, slot_source, entry
 
 
@@ -69,6 +69,8 @@
     rfright,
     zin,
     zout,
+    far_in,
+    far_out,
     lnv_all,
     lnv_cat,
     tile_matrix,
@@ -98,7 +100,8 @@
     cols = lax.axis_size("col")
     tiles = charge.shape[0]
     half = depth // 2
-    ob = dens.shape[1]
+    ob = phi.shape[1] // 3
+    hb = ob // 2
     z, x = lax.div(w, NX), lax.rem(w, NX)
 
     def chip(dz, dx):
@@ -129,43 +132,64 @@
         pl.semaphore_signal(barrier, inc=1, device_id=device, device_id_type=MESH)
     pl.semaphore_wait(barrier, len(greeted))
 
-    left0, right0, fleft0, fright0 = 4 * depth, 7 * depth, 10 * depth, 11 * depth
+    left0, right0, fleft0, fright0, far0 = 8 * depth, 13 * depth, 18 * depth, 19 * depth, 20 * depth
     span = 2 * depth
 
-    def z_copy(k, way, lo=0, hi=4):
+    def z_copy(chain, k, way, lo=0, hi=4):
+        stride, base = (8, 0) if chain == 0 else (8, 4) if chain == 1 else (4, far0)
         if way == 0:
-            j = lax.rem(depth - k, depth)
-            return remote(
-                buf.at[pl.ds(4 * j + lo, hi - lo)],
-                buf.at[pl.ds(4 * (depth - k - 1) + lo, hi - lo)],
-                z_sem, (0, k), zup,
-            )
+            src, dst = lax.rem(depth - k, depth), depth - k - 1
+        else:
+            src, dst = k, k + 1
         return remote(
-            buf.at[pl.ds(4 * k + lo, hi - lo)], buf.at[pl.ds(4 * k + 4 + lo, hi - lo)], z_sem, (1, k), zdn
+            buf.at[pl.ds(stride * src + base + lo, hi - lo)],
+            buf.at[pl.ds(stride * dst + base + lo, hi - lo)],
+            z_sem, (chain, way, k), (zup, zdn)[way],
         )
+
+    def z_first(chain):
+        for way in range(2):
+            z_copy(chain, 0, way).start()
+
+    def z_step(chain, k):
+        for way in range(2):
+            z_copy(chain, k - 1, way).wait_recv()
+            z_copy(chain, k, way).start()
+
+    def z_half(chain):
+        for way in range(2):
+            z_copy(chain, half - 2, way).wait_recv()
+            z_copy(chain, half - 1, way, 2 * way, 2 * way + 2).start()
+
+    def z_last(chain):
+        for way in range(2):
+            z_copy(chain, half - 1, way, 2 * way, 2 * way + 2).wait_recv()
 
     def x_copy(j, way):
         if way == 0:
-            return remote(xsend.at[0, j], buf.at[pl.ds(left0 + 3 * j, 3)], x_sem, (0, j), xr)
-        return remote(xsend.at[1, j], buf.at[pl.ds(right0 + 3 * j, 3)], x_sem, (1, j), xl)
+            return remote(xsend.at[0, j], buf.at[pl.ds(left0 + 5 * j, 5)], x_sem, (0, j), xr)
+        return remote(xsend.at[1, j], buf.at[pl.ds(right0 + 5 * j, 5)], x_sem, (1, j), xl)
 
     def f_copy(j, way):
         if way == 0:
-            return remote(buf.at[left0 + 3 * j + 2], buf.at[fleft0 + j], f_sem, (0, j), xr)
-        return remote(buf.at[right0 + 3 * j + 2], buf.at[fright0 + j], f_sem, (1, j), xl)
+            return remote(buf.at[left0 + 5 * j + 4], buf.at[fleft0 + j], f_sem, (0, j), xr)
+        return remote(buf.at[right0 + 5 * j + 4], buf.at[fright0 + j], f_sem, (1, j), xl)
 
     def pack(j):
         wanted = (((3, 0), (3, 1), (2, 0)), ((1, 0), (1, 1), (2, 1)))
-        for lo in range(0, ob, ROWS):
-            rows = pl.ds(lo, ROWS)
-            b = [buf[4 * j + s, rows, :].astype(jnp.float32) for s in range(4)]
-            for way in range(2):
-                for n, (dx, seat) in enumerate(wanted[way]):
-                    src = want[pl.ds(dx * span + 2 * j + seat, 1), :]
-                    got = jnp.where(
-                        src == 0, b[0], jnp.where(src == 1, b[1], jnp.where(src == 2, b[2], b[3]))
-                    )
-                    xsend[way, j, n, rows, :] = got.astype(jnp.bfloat16)
+        for h in range(2):
+            for lo in range(0, hb, ROWS):
+                rows = pl.ds(lo, ROWS)
+                b = [buf[8 * j + 4 * h + s, rows, :].astype(jnp.float32) for s in range(4)]
+                for way in range(2):
+                    for n, (dx, seat) in enumerate(wanted[way]):
+                        if n == 2 and h == 0:
+                            continue
+                        src = want[pl.ds(dx * span + 2 * j + seat, 1), :]
+                        got = jnp.where(
+                            src == 0, b[0], jnp.where(src == 1, b[1], jnp.where(src == 2, b[2], b[3]))
+                        )
+                        xsend[way, j, 4 if n == 2 else 2 * n + h, rows, :] = got.astype(jnp.bfloat16)
         for way in range(2):
             x_copy(j, way).start()
 
@@ -178,13 +202,15 @@
         rows = pl.ds(dx * span, span)
         return remote(req.at[rows], want.at[rows], want_sem, (dx,), device)
 
-    for s in range(4):
-        buf[s] = dens[s]
+    for s in range(8):
+        buf[s] = dens[s // 4 + 2 * (s % 4)]
     want_copies = [want_copy(1, xr), want_copy(3, xl), want_copy(2, x2)]
     for copy in want_copies:
         copy.start()
-    for way in range(2):
-        z_copy(0, way).start()
+    far_copy = remote(buf.at[pl.ds(0, 4)], buf.at[pl.ds(far0, 4)], want_sem, (0,), x2)
+    far_copy.start()
+    z_first(0)
+    z_first(1)
 
     def lnv_copy(d):
         return remote(lnv, lnv_all.at[pl.ds(4 * (cols - d), 4)], lnv_sem, (d,), strip[d - 1])
@@ -197,13 +223,15 @@
     for copy in want_copies:
         copy.wait_recv()
     pack(0)
+    far_copy.wait_recv()
+    z_first(2)
 
     def gather_step(k, carry):
-        for way in range(2):
-            z_copy(k - 1, way).wait_recv()
-            z_copy(k, way).start()
+        z_step(0, k)
+        z_step(1, k)
         pack(depth - k)
         pack(k)
+        z_step(2, k)
 
         @pl.when(k == 2)
         def _():
@@ -217,23 +245,24 @@
         return carry
 
     lax.fori_loop(1, half - 1, gather_step, 0)
-    for way in range(2):
-        z_copy(half - 2, way).wait_recv()
-        z_copy(half - 1, way, 2 * way, 2 * way + 2).start()
+    z_half(0)
+    z_half(1)
     pack(half + 1)
     pack(half - 1)
+    z_half(2)
     for k in range(half - 3, half - 1):
         if k == 0:
             forward(0)
         elif k > 0:
             forward(depth - k)
             forward(k)
-    for way in range(2):
-        z_copy(half - 1, way, 2 * way, 2 * way + 2).wait_recv()
+    z_last(0)
+    z_last(1)
     pack(half)
     forward(half + 1)
     forward(half - 1)
     forward(half)
+    z_last(2)
 
     def gather_end(j, carry):
         for way in range(2):
@@ -242,11 +271,39 @@
 
     lax.fori_loop(0, depth, gather_end, 0)
     phi_copy.wait()
+
+    def gather_sent():
+        def sent_x(j, carry):
+            for way in range(2):
+                x_copy(j, way).wait_send()
+                f_copy(j, way).wait_send()
+            return carry
+
+        def sent_z(k, carry):
+            for chain in range(3):
+                for way in range(2):
+                    z_copy(chain, k, way).wait_send()
+            return carry
+
+        for copy in want_copies:
+            copy.wait_send()
+        far_copy.wait_send()
+        for d in range(1, cols):
+            lnv_copy(d).wait_send()
+        for chain in range(3):
+            for way in range(2):
+                z_copy(chain, half - 1, way, 2 * way, 2 * way + 2).wait_send()
+        lax.fori_loop(0, depth, sent_x, 0)
+        lax.fori_loop(0, half - 1, sent_z, 0)
+
 
     def charge_step(t, carry):
         for a in range(3):
             for b in range(3):
-                tile_matrix[pl.ds(ob * a, ob), pl.ds(ob * b, ob)] = buf[entry[9 * t + 3 * a + b]]
+                for h in range(2):
+                    tile_matrix[pl.ds(ob * a + hb * h, hb), pl.ds(ob * b, ob)] = buf[
+                        entry[18 * t + 6 * a + 2 * b + h]
+                    ]
         values = phi[t]
         applied = jnp.dot(tile_matrix[...], values, preferred_element_type=jnp.float32)
         charge[pl.ds(t, 1), :] = jnp.sum(values.astype(jnp.float32) * applied, axis=0, keepdims=True)
@@ -325,6 +382,11 @@
     )
     pot_out[...] = partial + divergence / (2.0 * SPACING)
 
+    def halo_sent():
+        for n in range(4):
+            halo_copy(charge, halo, 0, n).wait_send()
+            halo_copy(flux.at[n // 2], halo2, 4, n).wait_send()
+
     parts[9 * tiles] = jnp.zeros((ob, ob), jnp.bfloat16)
 
     def part_step(t, carry):
@@ -345,18 +407,25 @@
 
     def rf_copy(j, way):
         return remote(
-            (rleft, rright)[way].at[j, 2], (rfleft, rfright)[way].at[j], rf_sem, (way, j), (xr, xl)[way]
+            (rleft, rright)[way].at[j, 4], (rfleft, rfright)[way].at[j], rf_sem, (way, j), (xr, xl)[way]
         )
 
-    def rz_copy(k, way, lo=0, hi=4):
+    def rz_copy(chain, k, way, lo=0, hi=4):
         rows = pl.ds(lo, hi - lo)
-        return remote(zout.at[way, k, rows], zin.at[way, k, rows], rz_sem, (way, k), (zup, zdn)[way])
+        return remote(
+            zout.at[way, k, chain, rows], zin.at[way, k, chain, rows], rz_sem, (chain, way, k), (zup, zdn)[way]
+        )
 
     def give(j):
         slots = (((1, 0), (1, 1), (2, 0)), ((3, 0), (3, 1), (2, 1)))
         for way in range(2):
             for n, (dx, seat) in enumerate(slots[way]):
-                rsend[way, j, n] = parts[slot_pair[dx * span + 2 * j + seat]]
+                pair = slot_pair[dx * span + 2 * j + seat]
+                if n < 2:
+                    rsend[way, j, 2 * n] = parts[pair, :hb, :]
+                    rsend[way, j, 2 * n + 1] = parts[pair, hb:, :]
+                else:
+                    rsend[way, j, 4] = parts[pair, hb:, :]
             rx_copy(j, way).start()
 
     def pass_on(j):
@@ -364,47 +433,90 @@
             rx_copy(j, way).wait_recv()
             rf_copy(j, way).start()
 
-    def summed(j, lo):
-        rows = pl.ds(lo, ROWS)
-        pieces = [
-            (0, 0, parts[slot_pair[2 * j], rows, :]),
-            (0, 1, parts[slot_pair[2 * j + 1], rows, :]),
-            (1, 0, rleft[j, 0, rows, :]),
-            (1, 1, rleft[j, 1, rows, :]),
-            (3, 0, rright[j, 0, rows, :]),
-            (3, 1, rright[j, 1, rows, :]),
-            (2, 0, rfleft[j, rows, :]),
-            (2, 1, rfright[j, rows, :]),
-        ]
+    def by_source(pieces, j):
         total = [jnp.zeros((ROWS, ob), jnp.float32)] * 4
-        for dx, seat, piece in pieces:
-            src = want[pl.ds(dx * span + 2 * j + seat, 1), :]
+        for ref, dx, seat, piece in pieces:
+            src = ref[pl.ds(dx * span + 2 * j + seat, 1), :]
             piece = piece.astype(jnp.float32)
             total = [t + jnp.where(src == s, piece, 0.0) for s, t in enumerate(total)]
         return total
 
+    def summed(j, chain, lo):
+        rows = pl.ds(lo, ROWS)
+        if chain == 2:
+            return by_source(
+                [(req, 2, s, parts[slot_pair[2 * span + 2 * j + s], rows, :]) for s in range(2)], j
+            )
+        pieces = [
+            (req, 0, s, parts[slot_pair[2 * j + s], pl.ds(hb * chain + lo, ROWS), :]) for s in range(2)
+        ]
+        for s in range(2):
+            pieces.append((want, 1, s, rleft[j, 2 * s + chain, rows, :]))
+            pieces.append((want, 3, s, rright[j, 2 * s + chain, rows, :]))
+        if chain == 1:
+            pieces.append((want, 2, 0, rfleft[j, rows, :]))
+            pieces.append((want, 2, 1, rfright[j, rows, :]))
+        return by_source(pieces, j)
+
     def arrived(j):
         for way in range(2):
             rf_copy(j, way).wait_recv()
 
-    for s in range(2):
-        zin[0, 0, 2 + s] = jnp.zeros((ob, ob), jnp.bfloat16)
-        zin[1, 0, s] = jnp.zeros((ob, ob), jnp.bfloat16)
+    def rz_first(chain):
+        for lo in range(0, hb, ROWS):
+            total = summed(half, chain, lo)
+            for s in range(4):
+                zout[s // 2, 0, chain, s, pl.ds(lo, ROWS), :] = total[s].astype(jnp.bfloat16)
+        for way in range(2):
+            rz_copy(chain, 0, way, 2 * way, 2 * way + 2).start()
+
+    def rz_arrived(chain, k, way):
+        @pl.when(k == 0)
+        def _():
+            rz_copy(chain, 0, way, 2 * way, 2 * way + 2).wait_recv()
+
+        @pl.when(k > 0)
+        def _():
+            rz_copy(chain, k, way).wait_recv()
+
+    def rz_step(chain, k, way):
+        j = half - k if way == 0 else half + k
+        rz_arrived(chain, k - 1, way)
+        for lo in range(0, hb, ROWS):
+            rows = pl.ds(lo, ROWS)
+            total = summed(j, chain, lo)
+            for s in range(4):
+                value = total[s] + zin[way, k - 1, chain, s, rows, :].astype(jnp.float32)
+                zout[way, k, chain, s, rows, :] = value.astype(jnp.bfloat16)
+        rz_copy(chain, k, way).start()
+
+    def rz_final(chain, lo):
+        rows = pl.ds(lo, ROWS)
+        return [
+            t + zin[0, half - 1, chain, s, rows, :].astype(jnp.float32)
+            + zin[1, half - 1, chain, s, rows, :].astype(jnp.float32)
+            for s, t in enumerate(summed(0, chain, lo))
+        ]
+
+    for chain in range(3):
+        for s in range(2):
+            zin[0, 0, chain, 2 + s] = jnp.zeros((hb, ob), jnp.bfloat16)
+            zin[1, 0, chain, s] = jnp.zeros((hb, ob), jnp.bfloat16)
     give(half)
+    rz_first(2)
     give(half - 1)
     give(half + 1)
     pass_on(half)
+    rz_first(0)
     give(half - 2)
     give(half + 2)
+    for way in range(2):
+        rz_step(2, 1, way)
     pass_on(half - 1)
     pass_on(half + 1)
     arrived(half)
-    for lo in range(0, ob, ROWS):
-        total = summed(half, lo)
-        for s in range(4):
-            zout[s // 2, 0, s, pl.ds(lo, ROWS), :] = total[s].astype(jnp.bfloat16)
-    for way in range(2):
-        rz_copy(0, way, 2 * way, 2 * way + 2).start()
+    rz_first(1)
+    far_sum_copy = remote(far_out, far_in, want_sem, (4,), x2)
 
     def reduce_step(k, carry):
         @pl.when(k < half - 2)
@@ -416,35 +528,29 @@
         def _():
             give(0)
 
+        for way in range(2):
+            rz_step(0, k, way)
+
         @pl.when(k < half - 1)
         def _():
+            for way in range(2):
+                rz_step(2, k + 1, way)
             pass_on(half - k - 1)
             pass_on(half + k + 1)
 
         @pl.when(k == half - 1)
         def _():
+            for way in range(2):
+                rz_arrived(2, half - 1, way)
+            for lo in range(0, hb, ROWS):
+                for s, value in enumerate(rz_final(2, lo)):
+                    far_out[s, pl.ds(lo, ROWS), :] = value.astype(jnp.bfloat16)
+            far_sum_copy.start()
             pass_on(0)
 
         for way in range(2):
-            j = half - k if way == 0 else half + k
-            arrived(j)
-
-            @pl.when(k == 1)
-            def _():
-                rz_copy(0, way, 2 * way, 2 * way + 2).wait_recv()
-
-            @pl.when(k > 1)
-            def _():
-                rz_copy(k - 1, way).wait_recv()
-
-            for lo in range(0, ob, ROWS):
-                rows = pl.ds(lo, ROWS)
-                total = summed(j, lo)
-                for s in range(4):
-                    zout[way, k, s, rows, :] = (
-                        total[s] + zin[way, k - 1, s, rows, :].astype(jnp.float32)
-                    ).astype(jnp.bfloat16)
-            rz_copy(k, way).start()
+            arrived(half - k if way == 0 else half + k)
+            rz_step(1, k, way)
         return carry
 
     lax.fori_loop(1, half, reduce_step, 0)
@@ -460,18 +566,37 @@
     lax.fori_loop(0, 4, left_step, 0)
     arrived(0)
     for way in range(2):
-        rz_copy(half - 1, way).wait_recv()
-    for lo in range(0, ob, ROWS):
-        rows = pl.ds(lo, ROWS)
-        total = summed(0, lo)
-        for s in range(4):
-            value = (
-                total[s]
-                + zin[0, half - 1, s, rows, :].astype(jnp.float32)
-                + zin[1, half - 1, s, rows, :].astype(jnp.float32)
-            )
-            ham_out[s, rows, :] = value
-            ham_half[s, rows, :] = value.astype(jnp.bfloat16)
+        rz_arrived(0, half - 1, way)
+        rz_arrived(1, half - 1, way)
+    far_sum_copy.wait_recv()
+    for chain in range(2):
+        for lo in range(0, hb, ROWS):
+            rows = pl.ds(hb * chain + lo, ROWS)
+            for s, value in enumerate(rz_final(chain, lo)):
+                if chain == 0:
+                    value = value + far_in[s, pl.ds(lo, ROWS), :].astype(jnp.float32)
+                ham_out[s, rows, :] = value
+                ham_half[s, rows, :] = value.astype(jnp.bfloat16)
+
+    def reduce_sent():
+        def sent_x(j, carry):
+            for way in range(2):
+                rx_copy(j, way).wait_send()
+                rf_copy(j, way).wait_send()
+            return carry
+
+        def sent_z(k, carry):
+            for chain in range(3):
+                for way in range(2):
+                    rz_copy(chain, k, way).wait_send()
+            return carry
+
+        for chain in range(3):
+            for way in range(2):
+                rz_copy(chain, 0, way, 2 * way, 2 * way + 2).wait_send()
+        far_sum_copy.wait_send()
+        lax.fori_loop(0, depth, sent_x, 0)
+        lax.fori_loop(1, half, sent_z, 0)
 
     def win_copy(src, dst, first, n):
         return remote(src, dst.at[pl.ds(8 * n, 4)], win_sem, (first + n,), (wp, wm)[n])
@@ -499,36 +624,12 @@
     for n in range(4):
         grad_out[n] = 3.0 * grad_out[n] - 2.0 * product(n, window2)
 
-    for copy in want_copies:
-        copy.wait_send()
-    for d in range(1, cols):
-        lnv_copy(d).wait_send()
-    for n in range(4):
-        halo_copy(charge, halo, 0, n).wait_send()
-        halo_copy(flux.at[n // 2], halo2, 4, n).wait_send()
+    gather_sent()
+    halo_sent()
+    reduce_sent()
     for n in range(2):
         win_copy(ham_half, window, 0, n).wait_send()
         win_copy(first_half, window2, 2, n).wait_send()
-    for way in range(2):
-        z_copy(half - 1, way, 2 * way, 2 * way + 2).wait_send()
-        rz_copy(0, way, 2 * way, 2 * way + 2).wait_send()
-
-    def sent_x(j, carry):
-        for way in range(2):
-            x_copy(j, way).wait_send()
-            f_copy(j, way).wait_send()
-            rx_copy(j, way).wait_send()
-            rf_copy(j, way).wait_send()
-        return carry
-
-    def sent_z(k, carry):
-        for way in range(2):
-            z_copy(k, way).wait_send()
-            rz_copy(k + 1, way).wait_send()
-        return carry
-
-    lax.fori_loop(0, depth, sent_x, 0)
-    lax.fori_loop(0, half - 1, sent_z, 0)
 
 
 def body(phi_values, density, lnv_matrix, core_density, pair_owner, pair_source, term_left, term_right):
@@ -547,6 +648,7 @@
         core_density.reshape(slabs, strips, tiles, deep // tiles).transpose(2, 0, 1, 3).reshape(tiles, points)
     )
     block = lambda *n: pltpu.VMEM((*n, ob, ob), jnp.bfloat16)
+    halves = lambda *n: pltpu.VMEM((*n, ob // 2, ob), jnp.bfloat16)
     sems = lambda *n: pltpu.SemaphoreType.DMA((2, *n))
     vmem = pl.BlockSpec(memory_space=pltpu.VMEM)
     smem = pl.BlockSpec(memory_space=pltpu.SMEM)
@@ -562,16 +664,18 @@
         scratch_shapes=[
             pltpu.VMEM(phi.shape, jnp.bfloat16),
             pltpu.VMEM(req.shape, jnp.int32),
-            block(12 * depth),
-            block(2, depth, 3),
+            halves(24 * depth),
+            halves(2, depth, 5),
             block(9 * tiles + 1),
-            block(2, depth, 3),
-            block(depth, 3),
-            block(depth, 3),
-            block(depth),
-            block(depth),
-            block(2, half, 4),
-            block(2, half, 4),
+            halves(2, depth, 5),
+            halves(depth, 5),
+            halves(depth, 5),
+            halves(depth),
+            halves(depth),
+            halves(2, half, 3, 4),
+            halves(2, half, 3, 4),
+            halves(4),
+            halves(4),
             block(4 * cols),
             pltpu.VMEM((4, ob, 8 * ob), jnp.bfloat16),
             pltpu.VMEM((3 * ob, 3 * ob), jnp.bfloat16),
@@ -584,14 +688,14 @@
             block(4),
             block(4),
             pltpu.SemaphoreType.DMA,
-            sems(4),
+            sems(5),
             sems(cols),
-            sems(2, half),
+            sems(3, 2, half),
             sems(2, depth),
             sems(2, depth),
             sems(2, depth),
             sems(2, depth),
-            sems(2, half),
+            sems(3, 2, half),
             sems(8),
             sems(4),
         ],
@@ -604,7 +708,7 @@
         left_at.reshape(-1),
         term_right.reshape(-1),
         req,
-        density.reshape(4, ob, ob),
+        density.reshape(8, ob // 2, ob),
         lnv_matrix.reshape(4, ob, ob),
         core,
         phi,

time: 162 us -> 145 us (0.90)
  Pallas kernels: 150 us -> 130 us
  other arithmetic: 2.49 us -> 4.61 us
    pallas_call x1, Pallas kernels: 150 us -> 130 us  [body(): pl.pallas_call(functools.partial(step_kernel, depth), out_shape=(jax.Shap...]
where the time goes in v2:
time: 145 us; the launch traced here: 143 us
  Pallas kernels  130 us (90%)
  local copies, waits for them, and re-layouts  7.99 us (6%)
  other arithmetic  4.61 us (3%)
    pallas_call x1, Pallas kernels, body(): pl.pallas_call(functools.partial(step_kernel, depth), out_shape=(jax.Shap...  130 us
    unnamed x8, local copies, waits for them, and re-layouts  5.09 us

profile of v2, /device:TPU:24, one launch (start us, length us, event | category | flops | bytes accessed | tf_op | source)
XLA Modules:
  0.0 143.2 jit_solution(2333456179146383620)
XLA Ops:
  0.7 0.8 reshape.262.right_at
  1.4 0.9 convert_reduce_fusion
  2.4 0.7 broadcast_compare_fusion.2
  3.1 0.7 broadcast_multiply_fusion
  3.7 0.8 fusion.3
  4.5 0.1 reshape.261.left_at
  4.6 0.7 multiply_add_fusion
  5.2 0.1 select_reduce_fusion
  5.4 0.8 select_select_fusion
  6.2 0.1 reshape.271.entry
  6.3 0.1 broadcast_in_dim.88.req
  6.4 0.8 reshape.265
  7.2 0.1 reshape.266.core
  7.4 0.0 copy-start
  7.4 1.9 %copy-done = bf16[1,1,8,384,512]{4,3,2,1,0:T(8,128)(2,1)S(1)} copy-done((bf16[1,1,8,384,512]{4,3,2,1,0:T(8,128)(2,1)S(1)}, bf16[1,1,8,384,512]{4,3,2,1,0:T(8,128)(2,1)}, u32[]{:S(2)}) %copy-start) | copy-done | bytes 3145752
  9.2 0.0 copy-start.1
  9.2 0.9 copy-done.1
  10.2 0.0 copy-start.2
  10.2 0.9 copy-done.2
  11.1 129.8 %shard_map.103 = (f32[8,512]{1,0:T(8,128)S(1)}, f32[4,128,128]{2,1,0:T(8,128)S(1)}, f32[4,128,128]{2,1,0:T(8,128)S(1)}) custom-call(s32[128]{0:T(128)S(1)} %get-tuple-element.23.slot_pair, s32[144]{0:T(256)S(1)} %reshape.271.entry, s32[32]{0:T(128)S(1)} %reshape.261.left_at, s32[32]{0:T(128)S(1)} %reshape.262.right_at, s32[128,128]{1,0:T(8,128)S(1)} %broadcast_in_dim.88.req, ...), custom_call_target="tpu_custom_call" | custom-call | tf_op jit(solution)/shard_map/pallas_call | solution.py:655
  140.9 0.1 reshape.267
  141.0 0.1 copy.16
  141.1 0.7 reshape.268
  141.8 0.7 copy.21
  142.5 0.7 copy.22
  (7 shorter events, 0.1 us)
Async XLA Ops:
  7.4 1.9 %copy-start = (bf16[1,1,8,384,512]{4,3,2,1,0:T(8,128)(2,1)S(1)}, bf16[1,1,8,384,512]{4,3,2,1,0:T(8,128)(2,1)}, u32[]{:S(2)}) copy-start(bf16[1,1,8,384,512]{4,3,2,1,0:T(8,128)(2,1)} %param.8) | copy-start | bytes 9437188
  9.2 0.9 copy-start.1
  10.2 0.9 copy-start.2

commit v3 on v2

--- a/solution.py
+++ b/solution.py
@@ -15,49 +15,68 @@
 MU = 0.2195
 FERMI_SQ = (3.0 * math.pi**2) ** (2.0 / 3.0)
 AMPLITUDE = 0.75 * (3.0 / math.pi) ** (1.0 / 3.0)
+VMEM_BYTES = 63 * 2**20
 ROWS = 32
 
 
-def place_arrays(owners, sources, depth):
-    me = lax.axis_index("wide")
-    pairs = owners.shape[0]
-    order = jnp.arange(pairs, dtype=jnp.int32)
-    dz = jnp.mod(owners // NX - me // NX, depth)
-    dx = jnp.mod(owners % NX - me % NX, NX)
-    same = (owners[:, None] == owners[None, :]) & (order[None, :] < order[:, None])
-    seat = jnp.sum(same.astype(jnp.int32), axis=1)
+def pair_places(owner, source, z, x, depth):
+    pairs = owner.shape[1]
+    slots = 2 * NX * depth
+    row = lax.broadcasted_iota(jnp.int32, (pairs, pairs), 0)
+    lane = lax.broadcasted_iota(jnp.int32, (pairs, pairs), 1)
+    along = owner
+    down = jnp.sum(jnp.where(row == lane, along, 0), axis=1, keepdims=True)
+    seat = jnp.sum(jnp.where((down == along) & (row < lane), 1, 0), axis=0, keepdims=True)
+    seat = jnp.minimum(seat, 1)
+    dz = lax.shift_right_logical(along, 2) - z
+    dz = jnp.where(dz < 0, dz + depth, dz)
+    dx = (along & 3) - x
+    dx = jnp.where(dx < 0, dx + NX, dx)
     slot = dx * (2 * depth) + dz * 2 + seat
-    slots = jnp.arange(2 * NX * depth, dtype=jnp.int32)
-    hit = slot[:, None] == slots[None, :]
-    slot_pair = jnp.sum(jnp.where(hit, order[:, None] - pairs, 0), axis=0) + pairs
-    slot_source = jnp.sum(jnp.where(hit, sources[:, None] + 1, 0), axis=0) - 1
-    part = jnp.arange(2, dtype=jnp.int32)[None, :]
-    dz, dx, seat, sources = dz[:, None], dx[:, None], seat[:, None], sources[:, None]
-    near = dz * 5 + seat * 2 + part
-    far = jnp.where(part == 0, 20 * depth + dz * 4 + sources, 18 * depth + seat * depth + dz)
-    entry = jnp.where(
-        dx == 0,
-        dz * 8 + part * 4 + sources,
-        jnp.where(dx == 3, 8 * depth + near, jnp.where(dx == 1, 13 * depth + near, far)),
-    ).reshape(-1)
-    return slot_pair, slot_source, entry
+    hit = slot == lax.broadcasted_iota(jnp.int32, (slots, pairs), 0)
+    slot_source = jnp.sum(jnp.where(hit, source + 1, 0), axis=1, keepdims=True) - 1
+    slot_down = jnp.sum(jnp.where(row == lane, slot, 0), axis=1, keepdims=True)
+    place = lax.broadcasted_iota(jnp.int32, (pairs, 128), 0)
+    hit = slot_down == lax.broadcasted_iota(jnp.int32, (pairs, 128), 1)
+    slot_pair = jnp.min(jnp.where(hit, place, pairs), axis=0, keepdims=True)
+    halves = []
+    for part in range(2):
+        near = dz * 5 + seat * 2 + part
+        far = 18 * depth + seat * depth + dz if part else 20 * depth + dz * 4 + source
+        halves.append(
+            jnp.where(
+                dx == 0,
+                dz * 8 + part * 4 + source,
+                jnp.where(dx == 3, 8 * depth + near, jnp.where(dx == 1, 13 * depth + near, far)),
+            )
+        )
+    return slot_source, slot_pair, halves
 
 
 def step_kernel(
     depth,
-    slot_pair,
-    entry,
-    left_at,
-    right_at,
-    req,
-    dens,
-    lnv,
-    core,
+    term_left,
+    term_right,
+    owner_hbm,
+    source_hbm,
+    dens_hbm,
+    lnv_hbm,
+    core_hbm,
     phi_hbm,
+    pot_hbm,
+    ham_hbm,
+    grad_hbm,
     pot_out,
     ham_out,
     grad_out,
+    owner,
+    source,
+    core_field,
+    core,
     phi,
+    places,
+    index,
+    req,
     want,
     buf,
     xsend,
@@ -78,11 +97,12 @@
     halo,
     flux,
     halo2,
+    pot,
     window,
     window2,
     ham_half,
     first_half,
-    phi_sem,
+    load_sem,
     want_sem,
     lnv_sem,
     z_sem,
@@ -93,6 +113,7 @@
     rz_sem,
     halo_sem,
     win_sem,
+    out_sem,
 ):
     w = lax.axis_index("wide")
     c = lax.axis_index("col")
@@ -107,11 +128,11 @@
     def chip(dz, dx):
         return (lax.rem(z + depth + dz, depth) * NX + lax.rem(x + NX + dx, NX), c)
 
+    slots = 2 * NX * depth
     zup, zdn, xr, xl, x2 = chip(1, 0), chip(-1, 0), chip(0, 1), chip(0, -1), chip(0, 2)
     wp = (lax.rem(w + 1, wides), c)
     wm = (lax.rem(w + wides - 1, wides), c)
-    strip = [(w, lax.rem(c + d, cols)) for d in range(1, cols)]
-    cp, cm = strip[0], strip[-1]
+    cp, cm = (w, lax.rem(c + 1, cols)), (w, lax.rem(c + cols - 1, cols))
 
     def remote(src, dst, sems, index, device):
         return pltpu.make_async_remote_copy(
@@ -123,13 +144,44 @@
             device_id_type=MESH,
         )
 
-    phi_copy = pltpu.make_async_copy(phi_hbm, phi, phi_sem)
-    phi_copy.start()
-
     barrier = pltpu.get_barrier_semaphore()
-    greeted = [zup, zdn, xr, xl, x2, wp, wm, *strip]
+    greeted = [zup, zdn, xr, xl, x2, wp, wm, cp, cm]
     for device in greeted:
         pl.semaphore_signal(barrier, inc=1, device_id=device, device_id_type=MESH)
+
+    loads = [
+        pltpu.make_async_copy(src, dst, load_sem.at[n])
+        for n, (src, dst) in enumerate(
+            (
+                (owner_hbm, owner),
+                (source_hbm, source),
+                (dens_hbm.at[:, 0], buf.at[pl.ds(0, 4)]),
+                (dens_hbm.at[:, 1], buf.at[pl.ds(4, 4)]),
+                (lnv_hbm, lnv_all.at[pl.ds(0, 4)]),
+                (core_hbm, core_field),
+                (phi_hbm, phi),
+            )
+        )
+    ]
+    for load in loads:
+        load.start()
+    loads[0].wait()
+    loads[1].wait()
+    slot_source, slot_pair_row, halves = pair_places(owner[...], source[...], z, x, depth)
+    req[...] = jnp.broadcast_to(slot_source, req.shape)
+    want[pl.ds(0, 2 * depth), :] = req[pl.ds(0, 2 * depth), :]
+    places[...] = jnp.zeros_like(places)
+    places[pl.ds(0, 1), :] = slot_pair_row
+    for part in range(2):
+        places[pl.ds(1 + part, 1), pl.ds(0, 9 * tiles)] = halves[part]
+    index_copy = pltpu.make_async_copy(places, index, load_sem.at[7])
+    index_copy.start()
+
+    def pair_of(dx, j, seat):
+        return index[0, dx * span + 2 * j + seat]
+
+    loads[2].wait()
+    loads[3].wait()
     pl.semaphore_wait(barrier, len(greeted))
 
     left0, right0, fleft0, fright0, far0 = 8 * depth, 13 * depth, 18 * depth, 19 * depth, 20 * depth
@@ -202,8 +254,6 @@
         rows = pl.ds(dx * span, span)
         return remote(req.at[rows], want.at[rows], want_sem, (dx,), device)
 
-    for s in range(8):
-        buf[s] = dens[s // 4 + 2 * (s % 4)]
     want_copies = [want_copy(1, xr), want_copy(3, xl), want_copy(2, x2)]
     for copy in want_copies:
         copy.start()
@@ -212,14 +262,18 @@
     z_first(0)
     z_first(1)
 
-    def lnv_copy(d):
-        return remote(lnv, lnv_all.at[pl.ds(4 * (cols - d), 4)], lnv_sem, (d,), strip[d - 1])
-
-    for d in range(1, cols):
-        lnv_copy(d).start()
-    for s in range(4):
-        lnv_all[s] = lnv[s]
-    want[pl.ds(0, span), :] = req[pl.ds(0, span), :]
+    turn = cols // 2
+
+    def lnv_copy(k, way):
+        lo, n = (2 * way, 2) if k == turn - 1 else (0, 4)
+        src, dst = ((cols - k) % cols, cols - k - 1) if way == 0 else (k, k + 1)
+        return remote(
+            lnv_all.at[pl.ds(4 * src + lo, n)], lnv_all.at[pl.ds(4 * dst + lo, n)], lnv_sem, (way, k), (cp, cm)[way]
+        )
+
+    loads[4].wait()
+    for way in range(2):
+        lnv_copy(0, way).start()
     for copy in want_copies:
         copy.wait_recv()
     pack(0)
@@ -232,6 +286,13 @@
         pack(depth - k)
         pack(k)
         z_step(2, k)
+        for n in range(1, turn):
+
+            @pl.when(k == n + 1)
+            def _():
+                for way in range(2):
+                    lnv_copy(n - 1, way).wait_recv()
+                    lnv_copy(n, way).start()
 
         @pl.when(k == 2)
         def _():
@@ -269,8 +330,26 @@
             f_copy(j, way).wait_recv()
         return carry
 
+    loads[5].wait()
+    field = core_field[...]
+    if field.shape[1] < 128:
+        field = jnp.pad(field, ((0, 0), (0, 128 - field.shape[1])))
+    group = lax.div(lax.broadcasted_iota(jnp.int32, (32, 128), 1), 16)
+    own_group = group[:8] == lax.broadcasted_iota(jnp.int32, (8, 128), 0)
+
+    def spread(a):
+        for shift in (64, 32, 16):
+            a = a + pltpu.roll(a, shift, 1)
+        return a
+
+    for t in range(tiles):
+        every = spread(jnp.where(group == t, field, 0.0))
+        for n in range(4):
+            chosen = jnp.where(own_group, every[8 * n : 8 * n + 8], 0.0)
+            core[pl.ds(t, 1), pl.ds(128 * n, 128)] = jnp.sum(chosen, axis=0, keepdims=True)
     lax.fori_loop(0, depth, gather_end, 0)
-    phi_copy.wait()
+    loads[6].wait()
+    index_copy.wait()
 
     def gather_sent():
         def sent_x(j, carry):
@@ -288,8 +367,9 @@
         for copy in want_copies:
             copy.wait_send()
         far_copy.wait_send()
-        for d in range(1, cols):
-            lnv_copy(d).wait_send()
+        for k in range(turn):
+            for way in range(2):
+                lnv_copy(k, way).wait_send()
         for chain in range(3):
             for way in range(2):
                 z_copy(chain, half - 1, way, 2 * way, 2 * way + 2).wait_send()
@@ -302,14 +382,14 @@
             for b in range(3):
                 for h in range(2):
                     tile_matrix[pl.ds(ob * a + hb * h, hb), pl.ds(ob * b, ob)] = buf[
-                        entry[18 * t + 6 * a + 2 * b + h]
+                        index[1 + h, 9 * t + 3 * a + b]
                     ]
         values = phi[t]
         applied = jnp.dot(tile_matrix[...], values, preferred_element_type=jnp.float32)
         charge[pl.ds(t, 1), :] = jnp.sum(values.astype(jnp.float32) * applied, axis=0, keepdims=True)
         return carry
 
-    lax.fori_loop(0, tiles, charge_step, 0)
+    lax.fori_loop(0, tiles, charge_step, 0, unroll=2)
 
     sides = (wp, wm, cp, cm)
 
@@ -380,7 +460,7 @@
         + y_prev(flux_y, halo2[2])
         - y_next(flux_y, halo2[3])
     )
-    pot_out[...] = partial + divergence / (2.0 * SPACING)
+    pot[...] = partial + divergence / (2.0 * SPACING)
 
     def halo_sent():
         for n in range(4):
@@ -391,7 +471,7 @@
 
     def part_step(t, carry):
         values = phi[t]
-        weighted = (values.astype(jnp.float32) * pot_out[pl.ds(t, 1), :]).astype(jnp.bfloat16)
+        weighted = (values.astype(jnp.float32) * pot[pl.ds(t, 1), :]).astype(jnp.bfloat16)
         block = lax.dot_general(
             weighted, values, (((1,), (1,)), ((), ())), preferred_element_type=jnp.float32
         ).astype(jnp.bfloat16)
@@ -400,7 +480,7 @@
                 parts[9 * t + 3 * a + b] = block[ob * a : ob * a + ob, ob * b : ob * b + ob]
         return carry
 
-    lax.fori_loop(0, tiles, part_step, 0)
+    lax.fori_loop(0, tiles, part_step, 0, unroll=2)
 
     def rx_copy(j, way):
         return remote(rsend.at[way, j], (rleft, rright)[way].at[j], rx_sem, (way, j), (xr, xl)[way])
@@ -420,7 +500,7 @@
         slots = (((1, 0), (1, 1), (2, 0)), ((3, 0), (3, 1), (2, 1)))
         for way in range(2):
             for n, (dx, seat) in enumerate(slots[way]):
-                pair = slot_pair[dx * span + 2 * j + seat]
+                pair = pair_of(dx, j, seat)
                 if n < 2:
                     rsend[way, j, 2 * n] = parts[pair, :hb, :]
                     rsend[way, j, 2 * n + 1] = parts[pair, hb:, :]
@@ -445,10 +525,10 @@
         rows = pl.ds(lo, ROWS)
         if chain == 2:
             return by_source(
-                [(req, 2, s, parts[slot_pair[2 * span + 2 * j + s], rows, :]) for s in range(2)], j
+                [(req, 2, s, parts[pair_of(2, j, s), rows, :]) for s in range(2)], j
             )
         pieces = [
-            (req, 0, s, parts[slot_pair[2 * j + s], pl.ds(hb * chain + lo, ROWS), :]) for s in range(2)
+            (req, 0, s, parts[pair_of(0, j, s), pl.ds(hb * chain + lo, ROWS), :]) for s in range(2)
         ]
         for s in range(2):
             pieces.append((want, 1, s, rleft[j, 2 * s + chain, rows, :]))
@@ -555,12 +635,23 @@
 
     lax.fori_loop(1, half, reduce_step, 0)
 
-    for d in range(1, cols):
-        lnv_copy(d).wait_recv()
+    for way in range(2):
+        lnv_copy(turn - 1, way).wait_recv()
+    for n in range(4):
+        slab = jnp.zeros((8, 128), jnp.float32)
+        for t in range(tiles):
+            points_t = jnp.broadcast_to(pot[pl.ds(t, 1), pl.ds(128 * n, 128)], (8, 128))
+            slab = jnp.where(group[:8] == t, spread(jnp.where(own_group, points_t, 0.0)), slab)
+        pot_out[pl.ds(8 * n, 8), :] = slab[:, : 16 * tiles]
+
+    pot_save = pltpu.make_async_copy(pot_out, pot_hbm, out_sem.at[0])
+    pot_save.start()
 
     def left_step(n, carry):
         for t in range(8):
-            lnv_cat[n, :, pl.ds(ob * t, ob)] = lnv_all[left_at[8 * n + t]]
+            slot = term_left[lax.div(n, 2), lax.rem(n, 2), t]
+            column = lax.rem(lax.shift_right_logical(slot, 1) + cols - c, cols)
+            lnv_cat[n, :, pl.ds(ob * t, ob)] = lnv_all[column * 4 + lax.div(n, 2) * 2 + (slot & 1)]
         return carry
 
     lax.fori_loop(0, 4, left_step, 0)
@@ -601,35 +692,60 @@
     def win_copy(src, dst, first, n):
         return remote(src, dst.at[pl.ds(8 * n, 4)], win_sem, (first + n,), (wp, wm)[n])
 
+    def win_block(s, n):
+        return remote(first_half.at[s], window2.at[8 * n + s], win_sem, (2 + 2 * s + n,), (wp, wm)[n])
+
     def product(n, win):
-        chosen = jnp.concatenate([win[right_at[8 * n + t]] for t in range(8)], axis=0)
+        chosen = jnp.concatenate([win[term_right[n // 2, n % 2, t]] for t in range(8)], axis=0)
         return jnp.dot(lnv_cat[n], chosen, preferred_element_type=jnp.float32)
 
     for n in range(2):
         win_copy(ham_half, window, 0, n).start()
+    ham_save = pltpu.make_async_copy(ham_out, ham_hbm, out_sem.at[1])
+    ham_save.start()
     for s in range(4):
         window[4 + s] = ham_half[s]
     for n in range(2):
         win_copy(ham_half, window, 0, n).wait_recv()
-    for n in range(4):
-        first = product(n, window)
-        grad_out[n] = first
-        first_half[n] = first.astype(jnp.bfloat16)
-    for n in range(2):
-        win_copy(first_half, window2, 2, n).start()
+    for s in range(4):
+        first = product(s, window)
+        grad_out[s] = first
+        first_half[s] = first.astype(jnp.bfloat16)
+        for n in range(2):
+            win_block(s, n).start()
     for s in range(4):
         window2[4 + s] = first_half[s]
-    for n in range(2):
-        win_copy(first_half, window2, 2, n).wait_recv()
-    for n in range(4):
-        grad_out[n] = 3.0 * grad_out[n] - 2.0 * product(n, window2)
+    for s in range(4):
+        for n in range(2):
+            win_block(s, n).wait_recv()
+    saves = [pot_save, ham_save]
+    for s in range(4):
+        grad_out[s] = 3.0 * grad_out[s] - 2.0 * product(s, window2)
+        saves.append(pltpu.make_async_copy(grad_out.at[s], grad_hbm.at[s], out_sem.at[2 + s]))
+        saves[-1].start()
 
     gather_sent()
     halo_sent()
     reduce_sent()
+    for save in saves:
+        save.wait()
     for n in range(2):
         win_copy(ham_half, window, 0, n).wait_send()
-        win_copy(first_half, window2, 2, n).wait_send()
+        for s in range(4):
+            win_block(s, n).wait_send()
+
+
+def save_kernel(*refs):
+    sources, results, held, sems = refs[:3], refs[3:6], refs[6:9], refs[9]
+    loads = [pltpu.make_async_copy(sources[n], held[n], sems.at[0, n]) for n in range(3)]
+    saves = [pltpu.make_async_copy(held[n], results[n], sems.at[1, n]) for n in range(3)]
+    for load in loads:
+        load.start()
+    for load, save in zip(loads, saves):
+        load.wait()
+        save.start()
+    for save in saves:
+        save.wait()
 
 
 def body(phi_values, density, lnv_matrix, core_density, pair_owner, pair_source, term_left, term_right):
@@ -639,31 +755,32 @@
     depth = lax.axis_size("wide") // NX
     cols = lax.axis_size("col")
     half = depth // 2
-    slot_pair, slot_source, entry = place_arrays(pair_owner[0, 0, :, 0], pair_source[0, 0], depth)
-    req = jnp.broadcast_to(slot_source[:, None], (2 * NX * depth, ob))
-    row = jnp.arange(2, dtype=jnp.int32)[:, None, None]
-    left_at = jnp.mod(term_left // 2 - lax.axis_index("col"), cols) * 4 + row * 2 + term_left % 2
     slabs, strips, deep = core_density.shape
-    core = (
-        core_density.reshape(slabs, strips, tiles, deep // tiles).transpose(2, 0, 1, 3).reshape(tiles, points)
+    slots = 2 * NX * depth
+    shapes = tuple(
+        jax.ShapeDtypeStruct(shape, jnp.float32) for shape in ((slabs * strips, deep), (4, ob, ob), (4, ob, ob))
     )
     block = lambda *n: pltpu.VMEM((*n, ob, ob), jnp.bfloat16)
     halves = lambda *n: pltpu.VMEM((*n, ob // 2, ob), jnp.bfloat16)
     sems = lambda *n: pltpu.SemaphoreType.DMA((2, *n))
-    vmem = pl.BlockSpec(memory_space=pltpu.VMEM)
     smem = pl.BlockSpec(memory_space=pltpu.SMEM)
-    pot, ham, grad = pl.pallas_call(
+    hbm = pl.BlockSpec(memory_space=pltpu.HBM)
+    outs = pl.pallas_call(
         functools.partial(step_kernel, depth),
-        out_shape=(
-            jax.ShapeDtypeStruct((tiles, points), jnp.float32),
-            jax.ShapeDtypeStruct((4, ob, ob), jnp.float32),
-            jax.ShapeDtypeStruct((4, ob, ob), jnp.float32),
-        ),
-        in_specs=[smem] * 4 + [vmem] * 4 + [pl.BlockSpec(memory_space=pl.ANY)],
-        out_specs=(vmem, vmem, vmem),
+        out_shape=shapes,
+        in_specs=[smem] * 2 + [hbm] * 6,
+        out_specs=(hbm, hbm, hbm),
         scratch_shapes=[
+            *[pltpu.VMEM(shape.shape, jnp.float32) for shape in shapes],
+            pltpu.VMEM((1, 9 * tiles), jnp.int32),
+            pltpu.VMEM((1, 9 * tiles), jnp.int32),
+            pltpu.VMEM((slabs * strips, deep), jnp.float32),
+            pltpu.VMEM((tiles, points), jnp.float32),
             pltpu.VMEM(phi.shape, jnp.bfloat16),
-            pltpu.VMEM(req.shape, jnp.int32),
+            pltpu.VMEM((8, 128), jnp.int32),
+            pltpu.SMEM((8, 128), jnp.int32),
+            pltpu.VMEM((slots, ob), jnp.int32),
+            pltpu.VMEM((slots, ob), jnp.int32),
             halves(24 * depth),
             halves(2, depth, 5),
             block(9 * tiles + 1),
@@ -683,13 +800,14 @@
             pltpu.VMEM((4, tiles, points), jnp.float32),
             pltpu.VMEM((2, tiles, points), jnp.float32),
             pltpu.VMEM((4, tiles, points), jnp.float32),
+            pltpu.VMEM((tiles, points), jnp.float32),
             block(12),
             block(12),
             block(4),
             block(4),
-            pltpu.SemaphoreType.DMA,
+            pltpu.SemaphoreType.DMA((8,)),
             sems(5),
-            sems(cols),
+            sems(2, cols // 2),
             sems(3, 2, half),
             sems(2, depth),
             sems(2, depth),
@@ -697,26 +815,30 @@
             sems(2, depth),
             sems(3, 2, half),
             sems(8),
-            sems(4),
+            sems(10),
+            pltpu.SemaphoreType.DMA((6,)),
         ],
         compiler_params=pltpu.CompilerParams(
-            collective_id=0, has_side_effects=True, vmem_limit_bytes=48 * 1024 * 1024
+            collective_id=0, has_side_effects=True, vmem_limit_bytes=VMEM_BYTES
         ),
     )(
-        slot_pair,
-        entry,
-        left_at.reshape(-1),
-        term_right.reshape(-1),
-        req,
-        density.reshape(8, ob // 2, ob),
+        term_left,
+        term_right,
+        pair_owner.reshape(1, 9 * tiles),
+        pair_source.reshape(1, 9 * tiles),
+        density.reshape(4, 2, ob // 2, ob),
         lnv_matrix.reshape(4, ob, ob),
-        core,
+        core_density.reshape(slabs * strips, deep),
         phi,
     )
-    potential = (
-        pot.reshape(tiles, slabs, strips, deep // tiles).transpose(1, 2, 0, 3).reshape(slabs, strips, deep)
-    )
-    return potential, ham.reshape(density.shape), grad.reshape(density.shape)
+    pot, ham, grad = pl.pallas_call(
+        save_kernel,
+        out_shape=shapes,
+        in_specs=[hbm] * 3,
+        out_specs=(hbm, hbm, hbm),
+        scratch_shapes=[*[pltpu.VMEM(shape.shape, jnp.float32) for shape in shapes], sems(3)],
+    )(*outs)
+    return pot.reshape(core_density.shape), ham.reshape(density.shape), grad.reshape(density.shape)
 
 
 def solution(mesh):

time: 145 us -> 133 us (0.917); the launches traced: 143 us -> 133 us
  local copies, waits for them, and re-layouts: 7.99 us -> 0 us
  other arithmetic: 4.61 us -> 0 us
  Pallas kernels: 130 us -> 132 us
    unnamed x8 -> x0, local copies, waits for them, and re-layouts: 5.09 us -> none
    reshape x7 -> x0, local copies, waits for them, and re-layouts: 2.6 us -> none  [the longest x3 0.96 us: body(): core_density.reshape(slabs, strips, tiles, deep // tiles)]
    pallas_call x1 -> x2, Pallas kernels: 130 us -> 132 us  [the longest x1 130 us: body(): pl.pallas_call(functools.partial(step_kernel, depth), out_shape=shapes, i...]
where the time goes in v3:
time: 133 us
  Pallas kernels  132 us (99%)
    pallas_call x1, Pallas kernels, body(): pl.pallas_call(functools.partial(step_kernel, depth), out_shape=shapes, i...  130 us

profile of v3, /device:TPU:24, one launch (start us, length us, event | category | flops | bytes accessed | tf_op | source)
XLA Modules:
  0.0 132.9 jit_solution(16548373235197969983)
XLA Ops:
  0.6 130.4 %shard_map.103 = (f32[32,128]{1,0:T(8,128)}, f32[4,128,128]{2,1,0:T(8,128)}, f32[4,128,128]{2,1,0:T(8,128)}) custom-call(s32[2,2,8]{2,1,0:T(2,128)} %term_left.1, s32[2,2,8]{2,1,0:T(2,128)} %term_right.1, s32[1,72]{1,0:T(1,128)} %bitcast.13, s32[1,72]{1,0:T(1,128)} %bitcast.14, bf16[4,2,64,128]{3,2,1,0:T(8,128)(2,1)} %bitcast.10, ...), custom_call_target="tpu_custom_call" | custom-call | tf_op jit(solution)/shard_map/pallas_call | solution.py:768
  131.1 1.8 %shard_map.104 = (f32[32,128]{1,0:T(8,128)}, f32[4,128,128]{2,1,0:T(8,128)}, f32[4,128,128]{2,1,0:T(8,128)}) custom-call(f32[32,128]{1,0:T(8,128)} %get-tuple-element.9.refs_0_, f32[4,128,128]{2,1,0:T(8,128)} %get-tuple-element.10.refs_1_, f32[4,128,128]{2,1,0:T(8,128)} %get-tuple-element.11.refs_2_), custom_call_target="tpu_custom_call" | custom-call | tf_op jit(solution)/shard_map/pallas_call | solution.py:834

commit v4 on v3

--- a/solution.py
+++ b/solution.py
@@ -294,14 +294,14 @@
                     lnv_copy(n - 1, way).wait_recv()
                     lnv_copy(n, way).start()
 
-        @pl.when(k == 2)
+        @pl.when(k == 1)
         def _():
             forward(0)
 
-        @pl.when(k > 2)
+        @pl.when(k > 1)
         def _():
-            forward(depth - k + 2)
-            forward(k - 2)
+            forward(depth - k + 1)
+            forward(k - 1)
 
         return carry
 
@@ -311,7 +311,7 @@
     pack(half + 1)
     pack(half - 1)
     z_half(2)
-    for k in range(half - 3, half - 1):
+    for k in range(half - 2, half - 1):
         if k == 0:
             forward(0)
         elif k > 0:
@@ -389,7 +389,7 @@
         charge[pl.ds(t, 1), :] = jnp.sum(values.astype(jnp.float32) * applied, axis=0, keepdims=True)
         return carry
 
-    lax.fori_loop(0, tiles, charge_step, 0, unroll=2)
+    lax.fori_loop(0, tiles, charge_step, 0, unroll=4)
 
     sides = (wp, wm, cp, cm)
 
@@ -480,7 +480,7 @@
                 parts[9 * t + 3 * a + b] = block[ob * a : ob * a + ob, ob * b : ob * b + ob]
         return carry
 
-    lax.fori_loop(0, tiles, part_step, 0, unroll=2)
+    lax.fori_loop(0, tiles, part_step, 0, unroll=4)
 
     def rx_copy(j, way):
         return remote(rsend.at[way, j], (rleft, rright)[way].at[j], rx_sem, (way, j), (xr, xl)[way])

time: 133 us -> 132 us (level)
    pallas_call x1, Pallas kernels: 130 us -> 129 us  [body(): pl.pallas_call(functools.partial(step_kernel, depth), out_shape=shapes, i...]
where the time goes in v4:
time: 132 us; the launch traced here: 131 us
  Pallas kernels  131 us (99%)
    pallas_call x1, Pallas kernels, body(): pl.pallas_call(functools.partial(step_kernel, depth), out_shape=shapes, i...  129 us

profile of v4, /device:TPU:24, one launch (start us, length us, event | category | flops | bytes accessed | tf_op | source)
XLA Modules:
  0.0 131.4 jit_solution(1967356853809947391)
XLA Ops:
  0.6 129.0 %shard_map.103 = (f32[32,128]{1,0:T(8,128)}, f32[4,128,128]{2,1,0:T(8,128)}, f32[4,128,128]{2,1,0:T(8,128)}) custom-call(s32[2,2,8]{2,1,0:T(2,128)} %term_left.1, s32[2,2,8]{2,1,0:T(2,128)} %term_right.1, s32[1,72]{1,0:T(1,128)} %bitcast.13, s32[1,72]{1,0:T(1,128)} %bitcast.14, bf16[4,2,64,128]{3,2,1,0:T(8,128)(2,1)} %bitcast.10, ...), custom_call_target="tpu_custom_call" | custom-call | tf_op jit(solution)/shard_map/pallas_call | solution.py:768
  129.6 1.8 %shard_map.104 = (f32[32,128]{1,0:T(8,128)}, f32[4,128,128]{2,1,0:T(8,128)}, f32[4,128,128]{2,1,0:T(8,128)}) custom-call(f32[32,128]{1,0:T(8,128)} %get-tuple-element.9.refs_0_, f32[4,128,128]{2,1,0:T(8,128)} %get-tuple-element.10.refs_1_, f32[4,128,128]{2,1,0:T(8,128)} %get-tuple-element.11.refs_2_), custom_call_target="tpu_custom_call" | custom-call | tf_op jit(solution)/shard_map/pallas_call | solution.py:834

commit v5 on v4

--- a/solution.py
+++ b/solution.py
@@ -655,12 +655,19 @@
         return carry
 
     lax.fori_loop(0, 4, left_step, 0)
-    arrived(0)
-    for way in range(2):
-        rz_arrived(0, half - 1, way)
-        rz_arrived(1, half - 1, way)
-    far_sum_copy.wait_recv()
+    def win_copy(chain, n):
+        rows = pl.ds(hb * chain, hb)
+        return remote(
+            ham_half.at[:, rows], window.at[pl.ds(8 * n, 4), rows], win_sem, (2 * chain + n,), (wp, wm)[n]
+        )
+
     for chain in range(2):
+        for way in range(2):
+            rz_arrived(chain, half - 1, way)
+        if chain == 0:
+            far_sum_copy.wait_recv()
+        else:
+            arrived(0)
         for lo in range(0, hb, ROWS):
             rows = pl.ds(hb * chain + lo, ROWS)
             for s, value in enumerate(rz_final(chain, lo)):
@@ -668,6 +675,8 @@
                     value = value + far_in[s, pl.ds(lo, ROWS), :].astype(jnp.float32)
                 ham_out[s, rows, :] = value
                 ham_half[s, rows, :] = value.astype(jnp.bfloat16)
+        for n in range(2):
+            win_copy(chain, n).start()
 
     def reduce_sent():
         def sent_x(j, carry):
@@ -689,24 +698,19 @@
         lax.fori_loop(0, depth, sent_x, 0)
         lax.fori_loop(1, half, sent_z, 0)
 
-    def win_copy(src, dst, first, n):
-        return remote(src, dst.at[pl.ds(8 * n, 4)], win_sem, (first + n,), (wp, wm)[n])
-
     def win_block(s, n):
-        return remote(first_half.at[s], window2.at[8 * n + s], win_sem, (2 + 2 * s + n,), (wp, wm)[n])
+        return remote(first_half.at[s], window2.at[8 * n + s], win_sem, (4 + 2 * s + n,), (wp, wm)[n])
 
     def product(n, win):
         chosen = jnp.concatenate([win[term_right[n // 2, n % 2, t]] for t in range(8)], axis=0)
         return jnp.dot(lnv_cat[n], chosen, preferred_element_type=jnp.float32)
 
-    for n in range(2):
-        win_copy(ham_half, window, 0, n).start()
     ham_save = pltpu.make_async_copy(ham_out, ham_hbm, out_sem.at[1])
     ham_save.start()
     for s in range(4):
         window[4 + s] = ham_half[s]
-    for n in range(2):
-        win_copy(ham_half, window, 0, n).wait_recv()
+    for n in range(4):
+        win_copy(n // 2, n % 2).wait_recv()
     for s in range(4):
         first = product(s, window)
         grad_out[s] = first
@@ -730,7 +734,8 @@
     for save in saves:
         save.wait()
     for n in range(2):
-        win_copy(ham_half, window, 0, n).wait_send()
+        for chain in range(2):
+            win_copy(chain, n).wait_send()
         for s in range(4):
             win_block(s, n).wait_send()
 
@@ -815,7 +820,7 @@
             sems(2, depth),
             sems(3, 2, half),
             sems(8),
-            sems(10),
+            sems(12),
             pltpu.SemaphoreType.DMA((6,)),
         ],
         compiler_params=pltpu.CompilerParams(

time: 132 us -> 132 us (level)
  no operation moved by 1% of the time
where the time goes in v5:
time: 132 us; the launch traced here: 131 us
  Pallas kernels  130 us (98%)
    pallas_call x1, Pallas kernels, body(): pl.pallas_call(functools.partial(step_kernel, depth), out_shape=shapes, i...  128 us

profile of v5, /device:TPU:24, one launch (start us, length us, event | category | flops | bytes accessed | tf_op | source)
XLA Modules:
  0.0 130.7 jit_solution(12023933145009348072)
XLA Ops:
  0.6 128.3 %shard_map.103 = (f32[32,128]{1,0:T(8,128)}, f32[4,128,128]{2,1,0:T(8,128)}, f32[4,128,128]{2,1,0:T(8,128)}) custom-call(s32[2,2,8]{2,1,0:T(2,128)} %term_left.1, s32[2,2,8]{2,1,0:T(2,128)} %term_right.1, s32[1,72]{1,0:T(1,128)} %bitcast.13, s32[1,72]{1,0:T(1,128)} %bitcast.14, bf16[4,2,64,128]{3,2,1,0:T(8,128)(2,1)} %bitcast.10, ...), custom_call_target="tpu_custom_call" | custom-call | tf_op jit(solution)/shard_map/pallas_call | solution.py:773
  128.9 1.8 %shard_map.104 = (f32[32,128]{1,0:T(8,128)}, f32[4,128,128]{2,1,0:T(8,128)}, f32[4,128,128]{2,1,0:T(8,128)}) custom-call(f32[32,128]{1,0:T(8,128)} %get-tuple-element.9.refs_0_, f32[4,128,128]{2,1,0:T(8,128)} %get-tuple-element.10.refs_1_, f32[4,128,128]{2,1,0:T(8,128)} %get-tuple-element.11.refs_2_), custom_call_target="tpu_custom_call" | custom-call | tf_op jit(solution)/shard_map/pallas_call | solution.py:839
